TPU v7x, 128 devices: a whole 4x4x4 slice. The times are simulated.
128 devices in a mesh: row: 8 (over y, core), col: 8 (over x, z_hi), chip: 2 (over z_lo).
Axes of the slice: x: 4, y: 4, z: 4 (z_hi: 2, z_lo: 2; z = z_hi * 2 + z_lo), core: 2. Of those that a mesh axis runs over, the one named last changes fastest.
Arguments:
- pair_input: float32 [512, 512, 128], P('row', ('col', 'chip')), may hold values from -8 to 8
- token_mask: int32 [512], replicated, may hold values from 0 to 1, as said below
- out_stack: bfloat16 [4, 128, 128], P(None, None, 'chip'), may hold values from -0.5 to 0.5
- out_gate: bfloat16 [128, 128], replicated, may hold values from -0.5 to 0.5
- out_final: bfloat16 [128, 128], P('chip'), may hold values from -0.5 to 0.5
- in_stack: bfloat16 [4, 128, 128], P(None, None, 'chip'), may hold values from -0.5 to 0.5
- in_gate: bfloat16 [128, 128], replicated, may hold values from -0.5 to 0.5
- in_final: bfloat16 [128, 128], P('chip'), may hold values from -0.5 to 0.5
- att_stack: bfloat16 [4, 128, 128], P(None, None, 'chip'), may hold values from -3 to 3
- att_bias: bfloat16 [128, 4], P(None, 'chip'), may hold values from -0.5 to 0.5
- att_out: bfloat16 [128, 128], P('chip'), may hold values from -0.5 to 0.5
Outputs:
- pair_output: float32 [512, 512, 128], P('row', ('col', 'chip'))
Inputs may be any that keep to these rules, and one draw needn't show every extreme that they name: `token_mask`: 1 on a leading run of tokens and 0 on a nonempty trailing run no longer than 64.
All inputs are finite; a program needn't handle non-finite values.
Results may differ from a plain program's by a relative error of at most 0.029.
Values may be sent and summed in bfloat16 or wider, within the bound.
A program may use at most 128 MiB of HBM per device.

v0:
```python
import jax
import jax.numpy as jnp
from jax import lax
from jax.sharding import PartitionSpec as P

epsilon = 1e-05


def from_root(value, axis, source):
    kept = jnp.where(lax.axis_index(axis) == source, value, 0).astype(value.dtype)
    return lax.psum(kept, axis)


def layer_norm(values):
    average = jnp.mean(values, axis=-1, keepdims=True)
    squares = jnp.mean(values * values, axis=-1, keepdims=True)
    return (values - average) * lax.rsqrt(squares - average * average + epsilon)


def normalize(pair_state):
    half_normed = layer_norm(pair_state).astype(jnp.bfloat16)
    normed = lax.all_gather(half_normed, "chip", axis=1, tiled=True)
    return (half_normed, normed)


def finish(hidden_part, final_weight):
    partial_value = jnp.einsum(
        "ijd,dc->ijc", hidden_part, final_weight, preferred_element_type=jnp.float32
    )
    return lax.psum_scatter(
        partial_value.astype(jnp.bfloat16), "chip", scatter_dimension=1, tiled=True
    ).astype(jnp.float32)


def triangle(pair_state, pair_mask, stack, gate_weight, final_weight, outgoing):
    half_normed, normed = normalize(pair_state)
    projected = jnp.einsum("ijc,scd->sijd", normed, stack, preferred_element_type=jnp.float32)
    first_arm = (jax.nn.sigmoid(projected[0]) * projected[1] * pair_mask[:, :, None]).astype(
        jnp.bfloat16
    )
    second_arm = (jax.nn.sigmoid(projected[2]) * projected[3] * pair_mask[:, :, None]).astype(
        jnp.bfloat16
    )
    gating = jax.nn.sigmoid(
        jnp.einsum("ijc,cd->ijd", half_normed, gate_weight, preferred_element_type=jnp.float32)
    )
    half_width = first_arm.shape[2]
    if outgoing:
        first_rows, second_rows = (
            lax.all_gather(first_arm, "col", axis=1, tiled=True),
            lax.all_gather(second_arm, "col", axis=1, tiled=True),
        )
        partner = from_root(second_rows, "row", lax.axis_index("col"))
        mixture = jnp.einsum(
            "ikd,jkd->ijd", first_rows, partner, preferred_element_type=jnp.float32
        )
    else:
        first_cols, second_cols = (
            lax.all_gather(first_arm, "row", axis=0, tiled=True),
            lax.all_gather(second_arm, "row", axis=0, tiled=True),
        )
        partner = from_root(first_cols, "col", lax.axis_index("row"))
        mixture = jnp.einsum(
            "kid,kjd->ijd", partner, second_cols, preferred_element_type=jnp.float32
        )
    width = half_width * lax.axis_size("chip")
    running, squares = (
        lax.psum(jnp.sum(mixture, axis=-1).astype(jnp.bfloat16), "chip").astype(jnp.float32),
        lax.psum(jnp.sum(mixture * mixture, axis=-1).astype(jnp.bfloat16), "chip").astype(
            jnp.float32
        ),
    )
    average = (running / width)[:, :, None]
    variance = (squares / width)[:, :, None] - average * average
    hidden = ((mixture - average) * lax.rsqrt(variance + epsilon)).astype(jnp.bfloat16)
    return pair_state + gating * finish(hidden, final_weight)


def attend(pair_state, token_mask, stack, bias_weight, out_weight):
    half_normed, normed = normalize(pair_state)
    projected = jnp.einsum("ijc,scd->sijd", normed, stack, preferred_element_type=jnp.float32)
    queries = projected[0].astype(jnp.bfloat16)
    key_proj = projected[1].astype(jnp.bfloat16)
    values = projected[2].astype(jnp.bfloat16)
    gating = jax.nn.sigmoid(projected[3])
    pair_bias = jnp.einsum(
        "ijc,ch->ijh", normed, bias_weight, preferred_element_type=jnp.float32
    ).astype(jnp.bfloat16)
    key_rows, value_rows, bias_rows = (
        lax.all_gather(key_proj, "col", axis=1, tiled=True),
        lax.all_gather(values, "col", axis=1, tiled=True),
        lax.all_gather(pair_bias, "col", axis=1, tiled=True),
    )
    bias_panel = from_root(bias_rows, "row", lax.axis_index("col"))
    tile_size = pair_bias.shape[0]
    head_count = pair_bias.shape[2]
    head_width = queries.shape[2] // head_count
    total_keys = key_rows.shape[1]
    bias_keys = jnp.transpose(bias_panel, (0, 2, 1)).astype(jnp.float32)
    key_live = token_mask > 0
    inv_root = head_width ** (-0.5)

    def score_block(first_row):
        q_block = lax.dynamic_slice_in_dim(queries, first_row, 8, 0).reshape(
            8, tile_size, head_count, head_width
        )
        k_block = lax.dynamic_slice_in_dim(key_rows, first_row, 8, 0).reshape(
            8, total_keys, head_count, head_width
        )
        v_block = lax.dynamic_slice_in_dim(value_rows, first_row, 8, 0).reshape(
            8, total_keys, head_count, head_width
        )
        scores = (
            jnp.einsum("ijhd,ikhd->ijhk", q_block, k_block, preferred_element_type=jnp.float32)
            * inv_root
            + bias_keys[None]
        )
        scores = jnp.where(key_live, scores, -1000000000.0)
        peaks = jnp.max(scores, axis=-1, keepdims=True)
        weights = jnp.exp(scores - peaks)
        weights = (weights / jnp.sum(weights, axis=-1, keepdims=True)).astype(jnp.bfloat16)
        attended = jnp.einsum(
            "ijhk,ikhd->ijhd", weights, v_block, preferred_element_type=jnp.float32
        )
        return attended.reshape(8, tile_size, head_count * head_width)

    block_starts = jnp.arange(tile_size // 8, dtype=jnp.int32) * 8
    attended = lax.map(score_block, block_starts).reshape(
        tile_size, tile_size, head_count * head_width
    )
    gated = (gating * attended).astype(jnp.bfloat16)
    return pair_state + finish(gated, out_weight)


def on_device(
    pair_input,
    token_mask,
    out_stack,
    out_gate,
    out_final,
    in_stack,
    in_gate,
    in_final,
    att_stack,
    att_bias,
    att_out,
):
    tile_size = pair_input.shape[0]
    row_mask = lax.dynamic_slice_in_dim(
        token_mask, lax.axis_index("row") * tile_size, tile_size
    ).astype(jnp.float32)
    col_mask = lax.dynamic_slice_in_dim(
        token_mask, lax.axis_index("col") * tile_size, tile_size
    ).astype(jnp.float32)
    pair_mask = row_mask[:, None] * col_mask[None, :]
    pair_state = triangle(pair_input, pair_mask, out_stack, out_gate, out_final, True)
    pair_state = triangle(pair_state, pair_mask, in_stack, in_gate, in_final, False)
    return attend(pair_state, token_mask, att_stack, att_bias, att_out)


def solution(mesh):
    return jax.shard_map(
        on_device,
        mesh=mesh,
        in_specs=(
            P("row", ("col", "chip"), None),
            P(),
            P(None, None, "chip"),
            P(),
            P("chip", None),
            P(None, None, "chip"),
            P(),
            P("chip", None),
            P(None, None, "chip"),
            P(None, "chip"),
            P("chip", None),
        ),
        out_specs=P("row", ("col", "chip"), None),
        check_vma=False,
    )
```

profile of v0, /device:TPU:1, one launch (start us, length us, event | category | flops | bytes accessed | tf_op | source)
XLA Modules:
  0.0 1253.4 jit_solution(12528048106480548369)
XLA Ops:
  6.5 1.9 fusion.78
  8.5 2.6 multiply_convert_fusion.2
  11.3 27.0 %all-gather.12.cloned.1.call-done = bf16[64,64,128]{2,1,0:T(8,128)(2,1)} async-done(((bf16[64,32,128]{2,1,0:T(8,128)(2,1)}), bf16[64,64,128]{2,1,0:T(8,128)(2,1)}) %all-gather.12.cloned.1.call-update) | async-done | bytes 1048592 | tf_op jit(solution)/shard_map/all_gather | solution.py:22
  38.4 2.5 convolution_bitcast_fusion.2
  40.9 2.3 fusion.32
  43.9 108.8 %all-gather.14.cloned.1.call-done = bf16[64,512,64]{2,1,0:T(8,128)(2,1)} async-done(((bf16[64,64,64]{2,1,0:T(8,128)(2,1)}), bf16[64,512,64]{2,1,0:T(8,128)(2,1)}) %all-gather.14.cloned.1.call-update) | async-done | bytes 4194320 | tf_op jit(solution)/shard_map/all_gather | solution.py:51
  152.8 3.8 broadcast_select_fusion
  156.6 105.2 %all-gather.16.cloned.1.call-done = bf16[64,512,64]{2,1,0:T(8,128)(2,1)} async-done(((bf16[64,64,64]{2,1,0:T(8,128)(2,1)}), bf16[64,512,64]{2,1,0:T(8,128)(2,1)}) %all-gather.16.cloned.1.call-update) | async-done | bytes 4194320 | tf_op jit(solution)/shard_map/all_gather | solution.py:50
  261.8 10.1 copy.34
  271.9 93.9 %all-reduce.6.cloned.1.call-done = bf16[64,512,64]{2,1,0:T(8,128)(2,1)} async-done(((bf16[64,512,64]{2,1,0:T(8,128)(2,1)}), bf16[64,512,64]{2,1,0:T(8,128)(2,1)}) %all-reduce.6.cloned.1.call-update) | async-done | bytes 4194320 | tf_op jit(solution)/shard_map/psum | solution.py:11
  365.7 10.1 copy.33
  375.8 4.7 bitcast_reduce_fusion.1
  380.5 6.4 all-reduce.1
  387.3 2.2 copy.35
  391.0 24.3 %reduce-scatter.4.cloned.1.call-done = bf16[64,32,128]{2,1,0:T(8,128)(2,1)} async-done(((bf16[64,64,128]{2,1,0:T(8,128)(2,1)}), bf16[64,32,128]{2,1,0:T(8,128)(2,1)}) %reduce-scatter.4.cloned.1.call-update) | async-done | bytes 524304 | tf_op jit(solution)/shard_map/reduce_scatter | solution.py:30
  415.3 2.4 fusion.77
  418.7 1.4 multiply_convert_fusion.1
  420.2 25.0 %all-gather.18.cloned.1.call-done = bf16[64,64,128]{2,1,0:T(8,128)(2,1)} async-done(((bf16[64,32,128]{2,1,0:T(8,128)(2,1)}), bf16[64,64,128]{2,1,0:T(8,128)(2,1)}) %all-gather.18.cloned.1.call-update) | async-done | bytes 1048592 | tf_op jit(solution)/shard_map/all_gather | solution.py:22
  445.2 2.5 convolution_bitcast_fusion.1
  447.7 2.3 fusion.20
  450.9 50.3 %all-gather.22.cloned.1.call-done = bf16[512,64,64]{2,1,0:T(8,128)(2,1)} async-done(((bf16[64,64,64]{2,1,0:T(8,128)(2,1)}), bf16[512,64,64]{2,1,0:T(8,128)(2,1)}) %all-gather.22.cloned.1.call-update) | async-done | bytes 4194320 | tf_op jit(solution)/shard_map/all_gather | solution.py:59
  501.2 12.1 copy.37
  513.3 2.4 broadcast_select_fusion.1
  515.8 37.2 %all-gather.20.cloned.1.call-done = bf16[512,64,64]{2,1,0:T(8,128)(2,1)} async-done(((bf16[64,64,64]{2,1,0:T(8,128)(2,1)}), bf16[512,64,64]{2,1,0:T(8,128)(2,1)}) %all-gather.20.cloned.1.call-update) | async-done | bytes 4194320 | tf_op jit(solution)/shard_map/all_gather | solution.py:60
  553.0 12.0 copy.38
  565.0 176.0 %all-reduce.8.cloned.1.call-done = bf16[512,64,64]{0,1,2:T(8,128)(2,1)} async-done(((bf16[512,64,64]{0,1,2:T(8,128)(2,1)}), bf16[512,64,64]{0,1,2:T(8,128)(2,1)}) %all-reduce.8.cloned.1.call-update) | async-done | bytes 4194320 | tf_op jit(solution)/shard_map/psum | solution.py:11
  741.1 4.7 bitcast_reduce_fusion
  745.8 5.8 all-reduce
  752.0 2.2 copy.39
  754.2 1.4 convolution_convert_fusion.1
  755.7 27.7 %reduce-scatter.6.cloned.1.call-done = bf16[64,32,128]{2,1,0:T(8,128)(2,1)} async-done(((bf16[64,64,128]{2,1,0:T(8,128)(2,1)}), bf16[64,32,128]{2,1,0:T(8,128)(2,1)}) %reduce-scatter.6.cloned.1.call-update) | async-done | bytes 524304 | tf_op jit(solution)/shard_map/reduce_scatter | solution.py:30
  783.5 2.4 fusion.76
  785.9 1.4 multiply_convert_fusion
  787.4 25.0 %all-gather.24.cloned.1.call-done = bf16[64,64,128]{2,1,0:T(8,128)(2,1)} async-done(((bf16[64,32,128]{2,1,0:T(8,128)(2,1)}), bf16[64,64,128]{2,1,0:T(8,128)(2,1)}) %all-gather.24.cloned.1.call-update) | async-done | bytes 1048592 | tf_op jit(solution)/shard_map/all_gather | solution.py:22
  812.4 2.2 convolution_convert_fusion.3
  814.7 28.2 %all_gather.39 = bf16[64,512,2]{0,2,1:T(2,128)(2,1)S(1)} all-gather(bf16[64,64,2]{0,2,1:T(2,128)(2,1)S(1)} %copy.41), channel_id=1, replica_groups=mesh['row'=8,'col'=8,'chip'=2] {'col'}, dimensions={1}, use_global_device_ids=true | all-gather | bytes 147456 | tf_op jit(solution)/shard_map/all_gather | solution.py:92
  844.0 4.6 fusion.80
  848.6 2.1 slice_bitcast_fusion.3
  851.6 57.1 %all-reduce.10.cloned.1.call-done = bf16[64,2,512]{0,1,2:T(2,128)(2,1)} async-done(((bf16[64,2,512]{0,1,2:T(2,128)(2,1)}), bf16[64,2,512]{0,1,2:T(2,128)(2,1)}) %all-reduce.10.cloned.1.call-update) | async-done | bytes 131088 | tf_op jit(solution)/shard_map/psum | solution.py:11
  908.7 1.8 copy.45
  910.5 110.5 %all-gather.26.cloned.1.call-done = bf16[1,64,512,64]{3,2,1,0:T(8,128)(2,1)} async-done(((bf16[1,64,64,64]{3,2,1,0:T(8,128)(2,1)}), bf16[1,64,512,64]{3,2,1,0:T(8,128)(2,1)}) %all-gather.26.cloned.1.call-update) | async-done | bytes 4194320 | tf_op jit(solution)/shard_map/all_gather | solution.py:91
  1021.0 8.5 copy.42
  1029.5 100.6 %all-gather.28.cloned.1.call-done = bf16[1,64,512,64]{3,2,1,0:T(8,128)(2,1)} async-done(((bf16[1,64,64,64]{3,2,1,0:T(8,128)(2,1)}), bf16[1,64,512,64]{3,2,1,0:T(8,128)(2,1)}) %all-gather.28.cloned.1.call-update) | async-done | bytes 4194320 | tf_op jit(solution)/shard_map/all_gather | solution.py:90
  1130.1 8.5 copy.43
  1138.7 80.6 %while.10 = (s32[]{:T(128)}, f32[8,8,64,64]{3,2,1,0:T(8,128)}, s32[8]{0:T(128)S(1)}, bf16[64,512,64]{1,2,0:T(8,128)(2,1)}, pred[512]{0:T(512)(128)(4,1)S(1)}, /*...) while((s32[]{:T(128)}, f32[8,8,64,64]{3,2,1,0:T(8,128)}, ...), condition=%wide.region_22.23_spmd, body=%wide.region_19.22_spmd.sunk | while | flops 70779392 | bytes 8725667 | solution.py:128
  1142.6 3.1 fusion.100
  1145.8 2.1 fusion.101
  1152.7 3.1 fusion.100
  1155.9 2.1 fusion.101
  1162.8 3.1 fusion.100
  1165.9 2.1 fusion.101
  1172.9 3.1 fusion.100
  1176.0 2.1 fusion.101
  1183.0 3.1 fusion.100
  1186.1 2.1 fusion.101
  1193.0 3.1 fusion.100
  1196.2 2.1 fusion.101
  1203.1 3.1 fusion.100
  1206.2 2.1 fusion.101
  1213.2 3.1 fusion.100
  1216.3 2.1 fusion.101
  1219.3 2.8 fusion.52
  1223.5 21.2 %reduce-scatter.8.cloned.1.call-done = bf16[64,32,128]{2,1,0:T(8,128)(2,1)} async-done(((bf16[64,64,128]{2,1,0:T(8,128)(2,1)}), bf16[64,32,128]{2,1,0:T(8,128)(2,1)}) %reduce-scatter.8.cloned.1.call-update) | async-done | bytes 524304 | tf_op jit(solution)/shard_map/reduce_scatter | solution.py:30
  1244.7 2.2 convert_add_fusion
  (124 shorter events, 32.1 us)
Async XLA Ops:
  6.5 837.4 %copy-start = (bf16[4,128,64]{1,2,0:T(8,128)(2,1)S(1)}, bf16[4,128,64]{1,2,0:T(8,128)(2,1)}, u32[]{:S(2)}) copy-start(bf16[4,128,64]{1,2,0:T(8,128)(2,1)} %param.21) | copy-start | bytes 196612
  6.5 4.6 copy-start.11
  6.5 31.8 %copy-start.6 = (bf16[4,128,64]{1,2,0:T(8,128)(2,1)S(1)}, bf16[4,128,64]{1,2,0:T(8,128)(2,1)}, u32[]{:S(2)}) copy-start(bf16[4,128,64]{1,2,0:T(8,128)(2,1)} %param.15) | copy-start | bytes 196612
  6.5 31.8 %all-gather.12.cloned.1.call-start = ((), (), s32[]{:S(2)}) async-start(), calls=%async_computation.3 | async-start | bytes 1572864 | tf_op jit(solution)/shard_map/all_gather | solution.py:22
  11.1 141.6 %all-gather.14.cloned.1.call-start = ((), (), s32[]{:S(2)}) async-start(), calls=%async_computation.4 | async-start | bytes 9437184 | tf_op jit(solution)/shard_map/all_gather | solution.py:51
  43.2 218.6 %all-gather.16.cloned.1.call-start = ((), (), s32[]{:S(2)}) async-start(), calls=%async_computation.6 | async-start | bytes 9437184 | tf_op jit(solution)/shard_map/all_gather | solution.py:50
  43.9 321.9 %all-reduce.6.cloned.1.call-start = ((), (), s32[]{:S(2)}) async-start(), calls=%async_computation.5 | async-start | bytes 16777216 | tf_op jit(solution)/shard_map/psum | solution.py:11
  156.6 258.7 %reduce-scatter.4.cloned.1.call-start = ((), (), s32[]{:S(2)}) async-start(), calls=%async_computation.7 | async-start | bytes 1572864 | tf_op jit(solution)/shard_map/reduce_scatter | solution.py:30
  387.0 2.6 copy-start.8
  389.6 25.7 %copy-start.2 = (f32[64,32,128]{2,1,0:T(8,128)S(1)}, f32[64,32,128]{2,1,0:T(8,128)}, u32[]{:S(2)}) copy-start(f32[64,32,128]{2,1,0:T(8,128)} %param.13) | copy-start | bytes 3145732
  389.6 25.7 %copy-start.13 = (bf16[128,128]{1,0:T(8,128)(2,1)S(1)}, bf16[128,128]{1,0:T(8,128)(2,1)}, u32[]{:S(2)}) copy-start(bf16[128,128]{1,0:T(8,128)(2,1)} %param.16) | copy-start | bytes 98308
  391.0 54.2 %all-gather.18.cloned.1.call-start = ((), (), s32[]{:S(2)}) async-start(), calls=%async_computation.8 | async-start | bytes 1572864 | tf_op jit(solution)/shard_map/all_gather | solution.py:22
  417.7 1.0 copy-start.4
  417.7 27.5 %copy-start.7 = (bf16[4,128,64]{1,2,0:T(8,128)(2,1)S(1)}, bf16[4,128,64]{1,2,0:T(8,128)(2,1)}, u32[]{:S(2)}) copy-start(bf16[4,128,64]{1,2,0:T(8,128)(2,1)} %param.18) | copy-start | bytes 196612
  420.1 81.1 %all-gather.22.cloned.1.call-start = ((), (), s32[]{:S(2)}) async-start(), calls=%async_computation.10 | async-start | bytes 9437184 | tf_op jit(solution)/shard_map/all_gather | solution.py:59
  450.0 103.0 %all-gather.20.cloned.1.call-start = ((), (), s32[]{:S(2)}) async-start(), calls=%async_computation.9 | async-start | bytes 9437184 | tf_op jit(solution)/shard_map/all_gather | solution.py:60
  450.7 290.4 %all-reduce.8.cloned.1.call-start = ((), (), s32[]{:S(2)}) async-start(), calls=%async_computation.11 | async-start | bytes 8388608 | tf_op jit(solution)/shard_map/psum | solution.py:11
  515.7 267.7 %reduce-scatter.6.cloned.1.call-start = ((), (), s32[]{:S(2)}) async-start(), calls=%async_computation.12 | async-start | bytes 1572864 | tf_op jit(solution)/shard_map/reduce_scatter | solution.py:30
  751.6 2.6 copy-start.9
  754.2 29.2 %copy-start.5 = (f32[64,32,128]{2,1,0:T(8,128)S(1)}, f32[64,32,128]{2,1,0:T(8,128)}, u32[]{:S(2)}) copy-start(f32[64,32,128]{2,1,0:T(8,128)} %copy-done.4) | copy-start | bytes 3145732
  754.2 29.2 %copy-start.14 = (bf16[128,128]{1,0:T(8,128)(2,1)S(1)}, bf16[128,128]{1,0:T(8,128)(2,1)}, u32[]{:S(2)}) copy-start(bf16[128,128]{1,0:T(8,128)(2,1)} %param.19) | copy-start | bytes 98308
  755.7 56.7 %all-gather.24.cloned.1.call-start = ((), (), s32[]{:S(2)}) async-start(), calls=%async_computation.13 | async-start | bytes 1572864 | tf_op jit(solution)/shard_map/all_gather | solution.py:22
  785.8 26.5 %copy-start.12 = (bf16[128,2]{0,1:T(2,128)(2,1)S(1)}, bf16[128,2]{0,1:T(2,128)(2,1)}, u32[]{:S(2)}) copy-start(bf16[128,2]{0,1:T(2,128)(2,1)} %param.22) | copy-start | bytes 1540
  787.3 121.4 %all-reduce.10.cloned.1.call-start = ((), (), s32[]{:S(2)}) async-start(), calls=%async_computation.14 | async-start | bytes 524288 | tf_op jit(solution)/shard_map/psum | solution.py:11
  812.4 31.6 %copy-start.3 = (bf16[64,64,128]{2,1,0:T(8,128)(2,1)S(1)}, bf16[64,64,128]{2,1,0:T(8,128)(2,1)}, u32[]{:S(2)}) copy-start(bf16[64,64,128]{2,1,0:T(8,128)(2,1)} %all-gather.24.cloned.1.call-done) | copy-start | bytes 3145732
  843.9 177.1 %all-gather.26.cloned.1.call-start = ((), (), s32[]{:S(2)}) async-start(), calls=%async_computation.16 | async-start | bytes 9437184 | tf_op jit(solution)/shard_map/all_gather | solution.py:91
  850.7 279.4 %all-gather.28.cloned.1.call-start = ((), (), s32[]{:S(2)}) async-start(), calls=%async_computation.17 | async-start | bytes 9437184 | tf_op jit(solution)/shard_map/all_gather | solution.py:90
  851.3 393.4 %reduce-scatter.8.cloned.1.call-start = ((), (), s32[]{:S(2)}) async-start(), calls=%async_computation.15 | async-start | bytes 1572864 | tf_op jit(solution)/shard_map/reduce_scatter | solution.py:30
  1219.3 2.8 copy-start.10
  1222.1 24.8 %copy-start.1 = (bf16[4,128,64]{1,2,0:T(8,128)(2,1)S(1)}, bf16[4,128,64]{1,2,0:T(8,128)(2,1)}, u32[]{:S(2)}) copy-start(bf16[4,128,64]{1,2,0:T(8,128)(2,1)} %param.21) | copy-start | bytes 196612
Sparse Core Ops, SparseCore 0:
  11.2 27.1 all-gather.11
  43.3 109.4 all-gather.13
  155.1 106.5 all-gather.15
  264.0 101.7 all-reduce.5
  391.1 24.1 reduce-scatter.3
  420.3 24.8 all-gather.17
  450.1 51.1 all-gather.21
  503.1 49.8 all-gather.19
  555.7 185.3 all-reduce.7
  755.8 27.6 reduce-scatter.5
  787.4 24.8 all-gather.23
  844.0 64.6 all-reduce.9
  911.3 109.6 all-gather.25
  1023.5 106.5 all-gather.27
  1223.6 21.0 reduce-scatter.7
where the time goes:
time: 1260 us; the launch traced here: 1250 us
  waiting for transfers between devices  992 us (79%)
  local copies, waits for them, and re-layouts  94.2 us (7%)
  matrix products  71.6 us (6%)
  blocking collectives  40.5 us (3%)
  other arithmetic  24.8 us (2%)
  loops' own time  15.8 us (1%)
  between operations  13.6 us (1%)
    psum x3, waiting for transfers between devices, from_root(): return lax.psum(kept, axis)  327 us
    all_gather x1, waiting for transfers between devices, attend(): lax.all_gather(values, 'col', axis=1, tiled=True)  110 us
    all_gather x1, waiting for transfers between devices, triangle(): lax.all_gather(second_arm, 'col', axis=1, tiled=True)  109 us
    all_gather x1, waiting for transfers between devices, triangle(): lax.all_gather(first_arm, 'col', axis=1, tiled=True)  105 us
    all_gather x1, waiting for transfers between devices, attend(): lax.all_gather(key_proj, 'col', axis=1, tiled=True)  101 us
    all_gather x3, waiting for transfers between devices, normalize(): normed = lax.all_gather(half_normed, 'chip', axis=1, tiled=True)  77 us
    reduce_scatter x3, waiting for transfers between devices, finish(): lax.psum_scatter(partial_value.astype(jnp.bfloat16), 'chip', scatter_dime...  73.2 us
    all_gather x1, waiting for transfers between devices, triangle(): lax.all_gather(first_arm, 'row', axis=0, tiled=True)  50.3 us
  transfers between devices with their start and end apart: 15, of which 15 were waited for; matrix products, arithmetic and copies ran while one was open for 5% of the time, Pallas kernels for 0%

commit v1 on v0

v1 whole, which is shorter than its diff:
```python
import functools
import math

import jax
import jax.numpy as jnp
from jax import lax
from jax.experimental import pallas as pl
from jax.experimental.pallas import tpu as pltpu
from jax.sharding import PartitionSpec as P

EPS = 1e-05
LOG2E = math.log2(math.e)
MESH = pl.DeviceIdType.MESH
BF = jnp.bfloat16
F32 = jnp.float32
ROWS = 4
GROUPS = 4
TILES = 8
STEP = 45


def dot(a, b, contract):
    return lax.dot_general(a, b, ((contract[:1], contract[1:]), ((), ())), preferred_element_type=F32)


def norm_columns(x):
    mean = jnp.mean(x, axis=0, keepdims=True)
    square = jnp.mean(x * x, axis=0, keepdims=True)
    return (x - mean) * lax.rsqrt(square - mean * mean + EPS)


def kernel(
    sizes,
    x_ref, tm_ref, os_ref, is_ref, as_ref, of_ref, if_ref, ao_ref, ab_ref, og_ref, ig_ref,
    out_ref,
    w_send, wall, w_gate, w_bias, w_fin, mask_o, mask_r,
    xs, xr, state, delta, gate, st_a, st_b, st_c,
    send_out, recv_out, back_out, home_out,
    send_in, recv_in, back_in, home_in,
    arm_a, arm_b,
    normed, bias_st, bias_send, bias_recv, bias_t,
    q_t, k_n, v_t, att, fin_send, fin_recv,
    send_sem, recv_sem,
):
    nr, nc, np_, heads = sizes
    ncp = nc * np_
    n_dev = nr * ncp
    n_ch = n_dev
    half = n_ch // 2
    hdev = n_dev // 2
    n_tok = ROWS * n_dev
    lanes = n_tok // GROUPS
    q_rows = ROWS * GROUPS
    n_pos = ROWS * n_tok
    width = n_pos // TILES
    per = width // lanes
    block_i = n_tok // nr
    block_j = n_tok // ncp
    h_dim = n_ch // heads
    r, c, p = lax.axis_index("row"), lax.axis_index("col"), lax.axis_index("chip")
    cp = c * np_ + p
    me = r * ncp + cp
    core, unit = lax.rem(r, 2), (r // 2) * ncp + cp

    barrier = pltpu.get_barrier_semaphore()

    def place(to):
        return to // ncp, lax.rem(to, ncp) // np_, lax.rem(to, np_)

    def greet(s, carry):
        to = lax.rem(me + s * STEP, n_dev)
        pl.semaphore_signal(barrier, inc=1, device_id=place(to), device_id_type=MESH)
        return carry

    lax.fori_loop(1, n_dev, greet, 0)

    def copy(src, dst, sem, to):
        return pltpu.make_async_remote_copy(
            src_ref=src, dst_ref=dst, send_sem=send_sem.at[sem], recv_sem=recv_sem.at[sem],
            device_id=place(to), device_id_type=MESH,
        )

    def drain(ref, sem):
        pltpu.make_async_copy(ref, ref, sem).wait()

    def span(t, size):
        return pl.ds(pl.multiple_of(t * size, size), size)

    n_first = 4 * half
    base = 3 * n_first
    for t, ref in enumerate((os_ref, is_ref, as_ref)):
        for s in range(4):
            rows = pl.ds((4 * t + s) * half, half)
            w_send[rows, :] = ref[s].astype(F32).T.astype(BF)
    for t, ref in enumerate((of_ref, if_ref, ao_ref)):
        w_send[base + t * half : base + (t + 1) * half, :] = ref[...]
    part = heads // 2
    w_send[base + 3 * half :, :] = jnp.concatenate(
        [ab_ref[...].astype(F32).T, jnp.zeros((16 - part, n_ch), F32)], axis=0
    ).astype(BF)
    wall[pl.ds(p, 1)] = w_send[...][None]
    for t, ref in enumerate((og_ref, ig_ref)):
        w_gate[t] = ref[...].astype(F32).T.astype(BF)

    live = tm_ref[...].astype(F32)
    token = lax.broadcasted_iota(jnp.int32, (lanes, n_tok), 1)
    lane = lax.broadcasted_iota(jnp.int32, (lanes, n_tok), 0)
    live_b = jnp.broadcast_to(live, (lanes, n_tok)).astype(BF)
    pick = (token == r * block_i + lax.rem(lane, block_i)).astype(F32).astype(BF)
    by_i = dot(live_b[:q_rows], pick, (1, 1))
    row_q = lax.broadcasted_iota(jnp.int32, (q_rows, n_tok), 0)
    token_q = lax.broadcasted_iota(jnp.int32, (q_rows, n_tok), 1)
    by_j = [
        dot((token_q == cp * block_j + e * q_rows + row_q).astype(F32).astype(BF), live_b, (1, 1))
        for e in range(2)
    ]
    lane_q = lax.broadcasted_iota(jnp.int32, (q_rows, lanes), 1)
    mask_o[...] = jnp.where(lane_q < block_i, by_j[0], by_j[1]) * by_i
    own = dot((token_q == me * ROWS + row_q // GROUPS).astype(F32).astype(BF), live_b, (1, 1))
    wide_live = jnp.concatenate(
        [live[:, g * lanes : (g + 1) * lanes] for g in range(GROUPS)] * ROWS, axis=0
    )
    mask_r[...] = own * wide_live

    xs[...] = x_ref[...].astype(BF)
    st_a[...] = x_ref[...].reshape(block_i * block_j, n_ch)

    def norm_input(t, carry):
        tile = jnp.concatenate(
            [
                st_a[pl.ds(e * q_rows + t * per + k, block_i, stride=block_j), :]
                for k in range(per)
                for e in range(2)
            ],
            axis=0,
        )
        normed[:, span(t, width)] = norm_columns(tile.T).astype(BF)
        return carry

    lax.fori_loop(0, TILES, norm_input, 0)

    def put_arms(w, h, tile, mask, t):
        proj = dot(w, tile, (1, 0))
        m = half
        first = jax.nn.sigmoid(proj[:m]) * proj[m : 2 * m] * mask
        second = jax.nn.sigmoid(proj[2 * m : 3 * m]) * proj[3 * m :] * mask
        for k in range(per):
            rows = pl.ds(h * (half * q_rows) + t * per + k, half, stride=q_rows)
            st_b[rows, :] = first[:, k * lanes : (k + 1) * lanes]
            st_c[rows, :] = second[:, k * lanes : (k + 1) * lanes]

    def mask_at(ref, t):
        return jnp.concatenate([ref[pl.ds(t * per + k, 1), :] for k in range(per)], axis=1)

    def pack(src, first, count, store):
        n = count // 8

        def body(t, carry):
            at = first + t * n
            rows = pl.ds(pl.multiple_of(at * q_rows, n * q_rows), n * q_rows)
            store(pl.ds(at, n), src[rows, :].reshape(n, q_rows, lanes).astype(BF))
            return carry

        lax.fori_loop(0, 8, body, 0)

    def pack_arms(send, first, count):
        def store_first(at, tile):
            send[at, 0] = tile

        def store_second(at, tile):
            send[at, 1] = tile

        pack(st_b, first, count, store_first)
        pack(st_c, first, count, store_second)

    def out_half(h):
        w = wall[pl.ds(h, 1), :n_first, :].reshape(n_first, n_ch)

        def body(t, carry):
            put_arms(w, h, normed[:, span(t, width)], mask_at(mask_o, t), t)
            return carry

        lax.fori_loop(0, TILES, body, 0)
        pack_arms(send_out, h * half, half)

    def send_half(h):
        def body(s, carry):
            to = h * hdev + lax.rem(me + s * STEP, hdev)
            copy(send_out.at[to], recv_out.at[me], 2, to).start()
            return carry

        lax.fori_loop(1, hdev, body, 0)

        @pl.when(me // hdev != h)
        def _():
            body(0, 0)

    out_half(p)
    pl.semaphore_wait(barrier, n_dev - 1)

    partner = r * ncp + c * np_ + lax.rem(p + 1, np_)
    w_early = copy(w_send.at[pl.ds(0, n_first)], wall.at[p, pl.ds(0, n_first)], 0, partner)
    w_early.start()
    n_late = w_send.shape[0] - n_first
    w_late = copy(w_send.at[pl.ds(n_first, n_late)], wall.at[p, pl.ds(n_first, n_late)], 8, partner)
    w_late.start()
    send_half(p)
    w_early.wait()
    out_half(1 - p)
    send_half(1 - p)

    def send_rows(s, carry):
        to_cp = lax.rem(cp + s, ncp)
        copy(
            xs.at[pl.ds(to_cp * ROWS, ROWS)], xr.at[:, pl.ds(cp * block_j, block_j), :], 1,
            r * ncp + to_cp,
        ).start()
        return carry

    lax.fori_loop(1, ncp, send_rows, 0)
    xr[:, pl.ds(cp * block_j, block_j), :] = xs[pl.ds(cp * ROWS, ROWS)]
    recv_out[pl.ds(me, 1)] = send_out[pl.ds(me, 1)]
    w_late.wait()
    for t in range(3):
        whole = jnp.concatenate(
            [wall[h, base + t * half : base + (t + 1) * half] for h in range(2)], axis=0
        )
        w_fin[t] = whole.astype(F32).T.astype(BF)
    w_bias[...] = jnp.concatenate(
        [wall[h, base + 3 * half : base + 3 * half + 16].astype(F32)[:part] for h in range(2)]
        + [jnp.zeros((8 - heads, n_ch), F32)],
        axis=0,
    ).astype(BF)
    drain(xs.at[pl.ds(0, (ncp - 1) * ROWS)], recv_sem.at[1])

    def load_state(t, carry):
        at = span(t, width)
        row, off = t // (TILES // ROWS), lax.rem(t, TILES // ROWS)
        tile = xr[row, span(off, width), :].astype(F32).T
        state[:, at] = tile
        gate[:, at] = jax.nn.sigmoid(dot(w_gate[0], norm_columns(tile).astype(BF), (1, 0)))
        return carry

    lax.fori_loop(0, TILES, load_state, 0)

    def unpack(load, dst):
        n = n_dev // 8

        def body(t, carry):
            tile = load(t, n).astype(F32).reshape(n * q_rows, lanes)
            dst[span(t, n * q_rows), :] = tile
            return carry

        lax.fori_loop(0, 8, body, 0)

    def all_to_all(src, dst, sem):
        def body(s, carry):
            to = lax.rem(me + s * STEP, n_dev)
            copy(src.at[to], dst.at[me], sem, to).start()
            return carry

        lax.fori_loop(1, n_dev, body, 0)
        dst[pl.ds(me, 1)] = src[pl.ds(me, 1)]

    def arrived(dst, sem):
        drain(dst.at[pl.ds(0, n_dev - 1)], recv_sem.at[sem])

    def update(t, which):
        at = span(t, width)
        hidden = jnp.concatenate(
            [st_a[pl.ds(t * per + k, n_ch, stride=q_rows), :] for k in range(per)], axis=1
        ).astype(BF)
        step = gate[:, at] * dot(w_fin[which], hidden, (1, 0))
        new = state[:, at] + step
        state[:, at] = new
        delta[:, at] = delta[:, at] + step if which else step
        return new

    def mix_and_return(outgoing, back, home, sem):
        n = n_tok // 4
        for m in range(4):
            mixed = dot(arm_a[:, m * n : (m + 1) * n], arm_b[...], (0, 0))
            for g in range(GROUPS):
                rows = pl.ds(m * n * GROUPS + g, n, stride=GROUPS)
                st_a[rows, :] = mixed[:, g * lanes : (g + 1) * lanes]

        def store_back(at, tile):
            back[at] = tile

        pack(st_a, 0, n_dev, store_back)
        all_to_all(back, home, sem)
        arrived(home, sem)
        m = n_dev // 8

        def sums(t, carry):
            tile = home[pl.ds(t * m, m)].astype(F32)
            return carry[0] + jnp.sum(tile, axis=0), carry[1] + jnp.sum(tile * tile, axis=0)

        zero = jnp.zeros((q_rows, lanes), F32)
        total, squares = lax.fori_loop(0, 8, sums, (zero, zero))
        mean = total / n_ch
        scale = lax.rsqrt(squares / n_ch - mean * mean + EPS)

        def normalize(t, carry):
            tile = (home[pl.ds(t * m, m)].astype(F32) - mean[None]) * scale[None]
            st_a[span(t, m * q_rows), :] = tile.reshape(m * q_rows, lanes)
            return carry

        lax.fori_loop(0, 8, normalize, 0)

    arrived(recv_out, 2)
    left = lax.broadcasted_iota(jnp.int32, (ncp * q_rows, lanes), 1) < block_i
    for a, dst in enumerate((arm_a, arm_b)):
        for m in range(nr // 2):
            tiles = [
                recv_out[(2 * m + k) * ncp : (2 * m + k + 1) * ncp, a]
                .astype(F32)
                .reshape(ncp * q_rows, lanes)
                for k in range(2)
            ]
            low = jnp.where(left, tiles[0], pltpu.roll(tiles[1], block_i, 1))
            high = jnp.where(left, pltpu.roll(tiles[0], block_i, 1), tiles[1])
            both = [y.reshape(ncp, 1, q_rows, lanes) for y in (low, high)]
            tile = jnp.concatenate(both, axis=1).reshape(n_tok, lanes)
            dst[:, m * lanes : (m + 1) * lanes] = tile.astype(BF)
    mix_and_return(True, back_out, home_out, 3)

    def project_in(t, carry):
        tile = norm_columns(update(t, 0)).astype(BF)
        mask = mask_at(mask_r, t)
        for h in range(2):
            put_arms(wall[h, n_first : 2 * n_first], h, tile, mask, t)
        gate[:, span(t, width)] = jax.nn.sigmoid(dot(w_gate[1], tile, (1, 0)))
        return carry

    lax.fori_loop(0, TILES, project_in, 0)
    pack_arms(send_in, 0, n_dev)
    all_to_all(send_in, recv_in, 4)
    arrived(recv_in, 4)
    unpack(lambda t, n: recv_in[pl.ds(t * n, n), 0], st_a)
    unpack(lambda t, n: recv_in[pl.ds(t * n, n), 1], st_b)
    for g in range(GROUPS):
        rows = pl.ds(g, n_tok, stride=GROUPS)
        arm_a[:, g * lanes : (g + 1) * lanes] = st_a[rows, :].astype(BF)
        arm_b[:, g * lanes : (g + 1) * lanes] = st_b[rows, :].astype(BF)
    mix_and_return(False, back_in, home_in, 5)

    def bias_step(t, carry):
        tile = norm_columns(update(t, 1)).astype(BF)
        normed[:, span(t, width)] = tile
        proj = dot(w_bias[...], tile, (1, 0)) * LOG2E
        for k in range(per):
            bias_st[pl.ds(t * per + k, 8, stride=q_rows), :] = proj[:, k * lanes : (k + 1) * lanes]
        return carry

    lax.fori_loop(0, TILES, bias_step, 0)
    bias_send[...] = bias_st[: heads * q_rows].astype(BF).reshape(heads, q_rows, lanes)
    for h in range(heads):

        def send_bias(s, carry, h=h):
            other = lax.rem(unit + s * STEP, hdev)
            to = ((other // ncp) * 2 + core) * ncp + lax.rem(other, ncp)
            copy(bias_send.at[h], bias_recv.at[h, core, unit], 10 + h, to).start()
            return carry

        lax.fori_loop(1, hdev, send_bias, 0)
        bias_recv[h, pl.ds(core, 1), pl.ds(unit, 1)] = bias_send[h][None, None]

    def qkvg(t, carry):
        at = span(t, width)
        tile = normed[:, at]
        row, off = t // (TILES // ROWS), lax.rem(t, TILES // ROWS)
        keys = []
        m = half
        for h in range(2):
            proj = dot(wall[h, 2 * n_first : 3 * n_first], tile, (1, 0))
            mine = slice(h * m, (h + 1) * m)
            q_t[mine, at] = (proj[:m] * (LOG2E * h_dim**-0.5)).astype(BF)
            keys.append(proj[m : 2 * m])
            v_t[mine, at] = proj[2 * m : 3 * m].astype(BF)
            gate[mine, at] = jax.nn.sigmoid(proj[3 * m :])
        k_n[row, span(off, width), :] = jnp.concatenate(keys, axis=0).T.astype(BF)
        return carry

    lax.fori_loop(0, TILES, qkvg, 0)
    sibling = (r + 1 - 2 * core) * ncp + cp
    wide = n_tok // 2

    def forward(h):
        drain(bias_recv.at[h, 0, pl.ds(0, hdev - 1)], recv_sem.at[10 + h])
        out = copy(bias_recv.at[h, core], bias_recv.at[h, core], 14 + h, sibling)
        out.start()
        return out

    def finish(i):
        for t in range(TILES // ROWS):
            at = pl.ds(pl.multiple_of(i * n_tok + t * width, width), width)
            gated = (gate[:, at] * att[:, at]).astype(BF)
            total = delta[:, at] + dot(w_fin[2], gated, (1, 0))
            fin_send[i, t * width : (t + 1) * width, :] = total.T.astype(BF)

        def send_final(s, carry):
            to_cp = lax.rem(cp + s, ncp)
            copy(
                fin_send.at[i, pl.ds(to_cp * block_j, block_j), :],
                fin_recv.at[cp * ROWS + i], 7, r * ncp + to_cp,
            ).start()
            return carry

        lax.fori_loop(1, ncp, send_final, 0)

    def attend(h):
        def load(t, n):
            return bias_recv[h, pl.ds(lax.rem(t, 2), 1), pl.ds(t // 2 * n, n)].reshape(n, q_rows, lanes)

        unpack(load, st_a)
        for g in range(GROUPS):
            tile = st_a[pl.ds(g, n_tok, stride=GROUPS), :]
            seen = tm_ref[:, g * lanes : (g + 1) * lanes] > 0
            bias_t[g * lanes : (g + 1) * lanes, :] = jnp.where(seen, tile, -1e30).T
        mine = slice(h * h_dim, (h + 1) * h_dim)

        def body(i, carry):
            keys = k_n[i]
            vals = jnp.concatenate([v_t[mine, span(i, n_tok)], jnp.ones((16, n_tok), BF)], axis=0)
            channel = lax.broadcasted_iota(jnp.int32, (n_ch, wide), 0)
            chosen = (channel >= h * h_dim) & (channel < (h + 1) * h_dim)
            for k in range(2):
                at = pl.ds(pl.multiple_of(i * n_tok + k * wide, wide), wide)
                query = jnp.where(chosen, q_t[:, at].astype(F32), 0.0).astype(BF)
                scores = dot(keys, query, (1, 0)) + bias_t[:, k * wide : (k + 1) * wide]
                peak = jnp.max(scores, axis=0, keepdims=True)
                weights = jnp.exp2(scores - peak).astype(BF)
                got = dot(vals, weights, (1, 0))
                att[mine, at] = got[:h_dim] / got[h_dim : h_dim + 1]
            if h == heads - 1:
                finish(i)
            return carry

        lax.fori_loop(0, ROWS, body, 0)

    forwards = [forward(0)]
    for h in range(heads):
        if h + 1 < heads:
            forwards.append(forward(h + 1))
        forwards[h].wait_recv()
        attend(h)

    fin_recv[pl.ds(cp * ROWS, ROWS)] = fin_send[:, pl.ds(cp * block_j, block_j), :]
    drain(fin_recv.at[pl.ds(0, (ncp - 1) * ROWS)], recv_sem.at[7])
    out_ref[...] = fin_recv[...]

    drain(xs.at[pl.ds(0, (ncp - 1) * ROWS)], send_sem.at[1])
    drain(send_out.at[pl.ds(0, n_dev - 1)], send_sem.at[2])
    drain(back_out.at[pl.ds(0, n_dev - 1)], send_sem.at[3])
    drain(send_in.at[pl.ds(0, n_dev - 1)], send_sem.at[4])
    drain(back_in.at[pl.ds(0, n_dev - 1)], send_sem.at[5])
    drain(fin_recv.at[pl.ds(0, (ncp - 1) * ROWS)], send_sem.at[7])
    for h in range(heads):
        drain(bias_recv.at[h, 0, pl.ds(0, hdev - 1)], send_sem.at[10 + h])
        forwards[h].wait_send()


def on_device(
    sizes, pair_input, token_mask,
    out_stack, out_gate, out_final, in_stack, in_gate, in_final, att_stack, att_bias, att_out,
):
    nr, nc, np_ = sizes
    heads = att_bias.shape[1] * np_
    n_dev = nr * nc * np_
    n_ch = n_dev
    n_tok = ROWS * n_dev
    lanes = n_tok // GROUPS
    q_rows = ROWS * GROUPS
    n_pos = ROWS * n_tok
    vm = pltpu.VMEM
    pair_t = (n_ch, n_pos)
    stage = (n_dev * q_rows, lanes)
    two = (n_dev, 2, q_rows, lanes)
    one = (n_dev, q_rows, lanes)
    w_rows = 15 * (n_ch // 2) + 16
    update = pl.pallas_call(
        functools.partial(kernel, (nr, nc, np_, heads)),
        out_shape=jax.ShapeDtypeStruct(pair_input.shape, BF),
        in_specs=[pl.BlockSpec(memory_space=pltpu.VMEM)] * 11,
        out_specs=pl.BlockSpec(memory_space=pltpu.VMEM),
        scratch_shapes=[
            vm((w_rows, n_ch), BF),
            vm((2, w_rows, n_ch), BF),
            vm((2, n_ch, n_ch), BF),
            vm((8, n_ch), BF),
            vm((3, n_ch, n_ch), BF),
            vm((q_rows, lanes), F32),
            vm((q_rows, lanes), F32),
            vm(pair_input.shape, BF),
            vm((ROWS, n_tok, n_ch), BF),
            vm(pair_t, F32),
            vm(pair_t, F32),
            vm(pair_t, F32),
            vm(stage, F32),
            vm(stage, F32),
            vm(stage, F32),
            vm(two, BF), vm(two, BF), vm(one, BF), vm(one, BF),
            vm(two, BF), vm(two, BF), vm(one, BF), vm(one, BF),
            vm((n_tok, n_tok), BF),
            vm((n_tok, n_tok), BF),
            vm(pair_t, BF),
            vm((8 * q_rows, lanes), F32),
            vm((heads, q_rows, lanes), BF),
            vm((heads, 2, n_dev // 2, q_rows, lanes), BF),
            vm((n_tok, n_tok), F32),
            vm(pair_t, BF),
            vm((ROWS, n_tok, n_ch), BF),
            vm(pair_t, BF),
            vm(pair_t, F32),
            vm((ROWS, n_tok, n_ch), BF),
            vm(pair_input.shape, BF),
            pltpu.SemaphoreType.DMA((18,)),
            pltpu.SemaphoreType.DMA((18,)),
        ],
        compiler_params=pltpu.CompilerParams(
            collective_id=0, has_side_effects=True, vmem_limit_bytes=56 * 2**20
        ),
        name="pair_update",
    )(
        pair_input, token_mask[None, :], out_stack, in_stack, att_stack,
        out_final, in_final, att_out, att_bias, out_gate, in_gate,
    )
    return pair_input + update.astype(F32)


def solution(mesh):
    sizes = tuple(mesh.shape[name] for name in ("row", "col", "chip"))
    return jax.shard_map(
        functools.partial(on_device, sizes),
        mesh=mesh,
        in_specs=(
            P("row", ("col", "chip"), None),
            P(),
            P(None, None, "chip"),
            P(),
            P("chip", None),
            P(None, None, "chip"),
            P(),
            P("chip", None),
            P(None, None, "chip"),
            P(None, "chip"),
            P("chip", None),
        ),
        out_specs=P("row", ("col", "chip"), None),
        check_vma=False,
    )
```

time: 1260 us -> 138 us (0.11)
  waiting for transfers between devices: 992 us -> 0 us
  Pallas kernels: 0 us -> 131 us
  local copies, waits for them, and re-layouts: 94.2 us -> 4.61 us
  matrix products: 71.6 us -> 0 us
  blocking collectives: 40.5 us -> 0 us
  other arithmetic: 24.8 us -> 2.17 us
  loops' own time: 15.8 us -> 0 us
  between operations: 13.6 us -> 0.02 us
    all_gather x9 -> x0, waiting for transfers between devices: 590 us -> none  [the longest x1 110 us: attend(): lax.all_gather(values, 'col', axis=1, tiled=True)]
    psum x3 -> x0, waiting for transfers between devices: 327 us -> none  [from_root(): return lax.psum(kept, axis)]
    pallas_call x0 -> x1, Pallas kernels: none -> 131 us  [on_device(): pl.pallas_call(functools.partial(kernel, (nr, nc, np_, heads)), out_shape...]
    reduce_scatter x3 -> x0, waiting for transfers between devices: 73.2 us -> none  [finish(): lax.psum_scatter(partial_value.astype(jnp.bfloat16), 'chip', scatter_dime...]
    dot_general x19 -> x0, matrix products: 46.5 us -> none  [the longest x8 16.4 us: score_block(): jnp.einsum('ijhk,ikhd->ijhd', weights, v_block, preferred_element_type=jn...]
    all_gather x3 -> x0, local copies, waits for them, and re-layouts: 34.2 us -> none  [the longest x1 12.1 us: triangle(): lax.all_gather(first_arm, 'row', axis=0, tiled=True)]
    all_gather x1 -> x0, blocking collectives: 28.2 us -> none  [attend(): lax.all_gather(pair_bias, 'col', axis=1, tiled=True)]
    sub x8 -> x0, matrix products: 25.1 us -> none  [score_block(): weights = jnp.exp(scores - peaks)]
  transfers between devices with their start and end apart: 15 -> 0, of which waited for: 15 -> 0; matrix products, arithmetic and copies ran while one was open for 5% -> 0% of each run, Pallas kernels for 0% -> 0%
where the time goes in v1:
time: 138 us
  Pallas kernels  131 us (95%)
  local copies, waits for them, and re-layouts  4.61 us (3%)
  other arithmetic  2.17 us (2%)
    pallas_call x1, Pallas kernels, on_device(): pl.pallas_call(functools.partial(kernel, (nr, nc, np_, heads)), out_shape...  131 us
    unnamed x12, local copies, waits for them, and re-layouts  4.61 us

profile of v1, /device:TPU:1, one launch (start us, length us, event | category | flops | bytes accessed | tf_op | source)
XLA Modules:
  0.0 137.8 jit_solution(9989205524549100083)
XLA Ops:
  0.0 0.0 copy-start.3
  0.0 0.7 copy-done.3
  0.7 0.7 copy.15.ab_ref
  1.4 0.0 copy-start.1
  1.4 1.6 %copy.12.os_ref = bf16[4,128,64]{2,1,0:T(8,128)(2,1)} copy(bf16[4,128,64]{1,2,0:T(8,128)(2,1)} %param.13) | data formatting | bytes 131072 | tf_op args[2]
  3.0 0.0 copy-done.1
  3.0 0.0 copy-start.2
  3.0 0.8 copy.13.is_ref
  3.8 0.1 copy-done.2
  3.9 0.8 copy.14.as_ref
  4.6 0.0 copy-start
  4.6 131.0 %pair_update.1 = bf16[64,32,128]{2,1,0:T(8,128)(2,1)} custom-call(f32[64,32,128]{2,1,0:T(8,128)} %x_ref.1, s32[1,512]{1,0:T(1,128)} %bitcast.1, bf16[4,128,64]{2,1,0:T(8,128)(2,1)} %copy.12.os_ref, bf16[4,128,64]{2,1,0:T(8,128)(2,1)} %copy.13.is_ref, bf16[4,128,64]{2,1,0:T(8,128)(2,1)} %copy.14.as_ref, bf16[64,128]{1,0:T(8,128)(2,1)} %of_ref.1, ...), custom_call_target="tpu_custom_call" | custom-call | tf_op jit(solution)/shard_map/pair_update/pallas_call | solution.py:482
  135.7 0.0 copy-done
  135.7 2.2 %convert_add_fusion = f32[64,32,128]{2,1,0:T(8,128)} fusion(f32[64,32,128]{2,1,0:T(8,128)S(1)} %copy-done, bf16[64,32,128]{2,1,0:T(8,128)(2,1)} %pair_update.1), kind=kLoop, calls=%fused_computation | loop fusion | flops 524288 | bytes 2621440 | tf_op jit(solution)/shard_map/add | solution.py:529
Async XLA Ops:
  0.0 0.7 copy-start.3
  1.4 1.6 %copy-start.1 = (bf16[4,128,64]{1,2,0:T(8,128)(2,1)S(1)}, bf16[4,128,64]{1,2,0:T(8,128)(2,1)}, u32[]{:S(2)}) copy-start(bf16[4,128,64]{1,2,0:T(8,128)(2,1)} %param.16) | copy-start | bytes 196612
  3.0 0.8 copy-start.2
  4.6 131.1 %copy-start = (f32[64,32,128]{2,1,0:T(8,128)S(1)}, f32[64,32,128]{2,1,0:T(8,128)}, u32[]{:S(2)}) copy-start(f32[64,32,128]{2,1,0:T(8,128)} %x_ref.1) | copy-start | bytes 3145732

commit v2 on v1

--- a/solution.py
+++ b/solution.py
@@ -67,12 +67,11 @@
     def place(to):
         return to // ncp, lax.rem(to, ncp) // np_, lax.rem(to, np_)
 
-    def greet(s, carry):
-        to = lax.rem(me + s * STEP, n_dev)
-        pl.semaphore_signal(barrier, inc=1, device_id=place(to), device_id_type=MESH)
-        return carry
-
-    lax.fori_loop(1, n_dev, greet, 0)
+    for s in range(1, n_dev):
+        s = s * STEP % n_dev
+        to_r = lax.rem(r + s // ncp, nr)
+        to = (to_r, lax.rem(c + s % ncp // np_, nc), lax.rem(p + s % np_, np_))
+        pl.semaphore_signal(barrier, inc=1, device_id=to, device_id_type=MESH)
 
     def copy(src, dst, sem, to):
         return pltpu.make_async_remote_copy(
@@ -91,12 +90,12 @@
     for t, ref in enumerate((os_ref, is_ref, as_ref)):
         for s in range(4):
             rows = pl.ds((4 * t + s) * half, half)
-            w_send[rows, :] = ref[s].astype(F32).T.astype(BF)
+            w_send[rows, :] = ref[s]
     for t, ref in enumerate((of_ref, if_ref, ao_ref)):
         w_send[base + t * half : base + (t + 1) * half, :] = ref[...]
     part = heads // 2
     w_send[base + 3 * half :, :] = jnp.concatenate(
-        [ab_ref[...].astype(F32).T, jnp.zeros((16 - part, n_ch), F32)], axis=0
+        [ab_ref[...].astype(F32), jnp.zeros((16 - part, n_ch), F32)], axis=0
     ).astype(BF)
     wall[pl.ds(p, 1)] = w_send[...][None]
     for t, ref in enumerate((og_ref, ig_ref)):
@@ -153,7 +152,7 @@
         return jnp.concatenate([ref[pl.ds(t * per + k, 1), :] for k in range(per)], axis=1)
 
     def pack(src, first, count, store):
-        n = count // 8
+        n = max(count // 8, 1)
 
         def body(t, carry):
             at = first + t * n
@@ -161,7 +160,7 @@
             store(pl.ds(at, n), src[rows, :].reshape(n, q_rows, lanes).astype(BF))
             return carry
 
-        lax.fori_loop(0, 8, body, 0)
+        lax.fori_loop(0, count // n, body, 0)
 
     def pack_arms(send, first, count):
         def store_first(at, tile):
@@ -198,16 +197,30 @@
     out_half(p)
     pl.semaphore_wait(barrier, n_dev - 1)
 
-    partner = r * ncp + c * np_ + lax.rem(p + 1, np_)
-    w_early = copy(w_send.at[pl.ds(0, n_first)], wall.at[p, pl.ds(0, n_first)], 0, partner)
-    w_early.start()
-    n_late = w_send.shape[0] - n_first
-    w_late = copy(w_send.at[pl.ds(n_first, n_late)], wall.at[p, pl.ds(n_first, n_late)], 8, partner)
-    w_late.start()
+    n_z = 2 * min(nc, 2)
+    z = lax.rem(c, 2) * np_ + p if nc > 1 else p
+    ways = []
+    for step in (1, n_z - 1):
+        to_z = lax.rem(z + step, n_z)
+        to_c = c // 2 * 2 + to_z // np_ if nc > 1 else c
+        ways.append(r * ncp + to_c * np_ + lax.rem(to_z, np_))
+
+    def give(first, count, sem):
+        cut = count // 32 * 16
+        both = []
+        for k, (at, n) in enumerate(((first, cut), (first + cut, count - cut))):
+            rows = pl.ds(at, n)
+            both.append(copy(w_send.at[rows], wall.at[p, rows], sem + k, ways[k]))
+            both[k].start()
+        return both
+
+    early = give(0, n_first, 8)
     send_half(p)
-    w_early.wait()
+    for w_copy in early:
+        w_copy.wait()
     out_half(1 - p)
     send_half(1 - p)
+    late = give(n_first, w_send.shape[0] - n_first, 18)
 
     def send_rows(s, carry):
         to_cp = lax.rem(cp + s, ncp)
@@ -220,28 +233,31 @@
     lax.fori_loop(1, ncp, send_rows, 0)
     xr[:, pl.ds(cp * block_j, block_j), :] = xs[pl.ds(cp * ROWS, ROWS)]
     recv_out[pl.ds(me, 1)] = send_out[pl.ds(me, 1)]
-    w_late.wait()
-    for t in range(3):
-        whole = jnp.concatenate(
-            [wall[h, base + t * half : base + (t + 1) * half] for h in range(2)], axis=0
-        )
-        w_fin[t] = whole.astype(F32).T.astype(BF)
-    w_bias[...] = jnp.concatenate(
-        [wall[h, base + 3 * half : base + 3 * half + 16].astype(F32)[:part] for h in range(2)]
-        + [jnp.zeros((8 - heads, n_ch), F32)],
-        axis=0,
-    ).astype(BF)
-    drain(xs.at[pl.ds(0, (ncp - 1) * ROWS)], recv_sem.at[1])
-
-    def load_state(t, carry):
-        at = span(t, width)
-        row, off = t // (TILES // ROWS), lax.rem(t, TILES // ROWS)
-        tile = xr[row, span(off, width), :].astype(F32).T
-        state[:, at] = tile
-        gate[:, at] = jax.nn.sigmoid(dot(w_gate[0], norm_columns(tile).astype(BF), (1, 0)))
-        return carry
-
-    lax.fori_loop(0, TILES, load_state, 0)
+
+    def load_rows():
+        for w_copy in late:
+            w_copy.wait()
+        for t in range(3):
+            whole = jnp.concatenate(
+                [wall[h, base + t * half : base + (t + 1) * half] for h in range(2)], axis=0
+            )
+            w_fin[t] = whole.astype(F32).T.astype(BF)
+        w_bias[...] = jnp.concatenate(
+            [wall[h, base + 3 * half : base + 3 * half + 16].astype(F32)[:part] for h in range(2)]
+            + [jnp.zeros((8 - heads, n_ch), F32)],
+            axis=0,
+        ).astype(BF)
+        drain(xs.at[pl.ds(0, (ncp - 1) * ROWS)], recv_sem.at[1])
+
+        def load_state(t, carry):
+            at = span(t, width)
+            row, off = t // (TILES // ROWS), lax.rem(t, TILES // ROWS)
+            tile = xr[row, span(off, width), :].astype(F32).T
+            state[:, at] = tile
+            gate[:, at] = jax.nn.sigmoid(dot(w_gate[0], norm_columns(tile).astype(BF), (1, 0)))
+            return carry
+
+        lax.fori_loop(0, TILES, load_state, 0)
 
     def unpack(load, dst):
         n = n_dev // 8
@@ -252,15 +268,6 @@
             return carry
 
         lax.fori_loop(0, 8, body, 0)
-
-    def all_to_all(src, dst, sem):
-        def body(s, carry):
-            to = lax.rem(me + s * STEP, n_dev)
-            copy(src.at[to], dst.at[me], sem, to).start()
-            return carry
-
-        lax.fori_loop(1, n_dev, body, 0)
-        dst[pl.ds(me, 1)] = src[pl.ds(me, 1)]
 
     def arrived(dst, sem):
         drain(dst.at[pl.ds(0, n_dev - 1)], recv_sem.at[sem])
@@ -276,19 +283,29 @@
         delta[:, at] = delta[:, at] + step if which else step
         return new
 
-    def mix_and_return(outgoing, back, home, sem):
+    def mix_and_return(arm_chunk, back, home, sem, meanwhile):
         n = n_tok // 4
-        for m in range(4):
-            mixed = dot(arm_a[:, m * n : (m + 1) * n], arm_b[...], (0, 0))
+        n_to = n_dev // 4
+        for k in range(4):
+            m = lax.rem(r // 2 + k, 4)
+            mixed = dot(arm_chunk(m), arm_b[...], (0, 0))
             for g in range(GROUPS):
-                rows = pl.ds(m * n * GROUPS + g, n, stride=GROUPS)
-                st_a[rows, :] = mixed[:, g * lanes : (g + 1) * lanes]
-
-        def store_back(at, tile):
-            back[at] = tile
-
-        pack(st_a, 0, n_dev, store_back)
-        all_to_all(back, home, sem)
+                rows = pl.ds(m * (n * GROUPS) + g, n, stride=GROUPS)
+                st_c[rows, :] = mixed[:, g * lanes : (g + 1) * lanes]
+
+            def store_back(at, tile):
+                back[at] = tile
+
+            pack(st_c, m * n_to, n_to, store_back)
+
+            def body(s, carry, m=m):
+                to = m * n_to + lax.rem(me + s * STEP, n_to)
+                copy(back.at[to], home.at[me], sem, to).start()
+                return carry
+
+            lax.fori_loop(0 if k else 1, n_to, body, 0)
+        home[pl.ds(me, 1)] = back[pl.ds(me, 1)]
+        meanwhile()
         arrived(home, sem)
         m = n_dev // 8
 
@@ -310,32 +327,55 @@
 
     arrived(recv_out, 2)
     left = lax.broadcasted_iota(jnp.int32, (ncp * q_rows, lanes), 1) < block_i
-    for a, dst in enumerate((arm_a, arm_b)):
-        for m in range(nr // 2):
-            tiles = [
-                recv_out[(2 * m + k) * ncp : (2 * m + k + 1) * ncp, a]
-                .astype(F32)
-                .reshape(ncp * q_rows, lanes)
-                for k in range(2)
-            ]
-            low = jnp.where(left, tiles[0], pltpu.roll(tiles[1], block_i, 1))
-            high = jnp.where(left, pltpu.roll(tiles[0], block_i, 1), tiles[1])
-            both = [y.reshape(ncp, 1, q_rows, lanes) for y in (low, high)]
-            tile = jnp.concatenate(both, axis=1).reshape(n_tok, lanes)
-            dst[:, m * lanes : (m + 1) * lanes] = tile.astype(BF)
-    mix_and_return(True, back_out, home_out, 3)
-
-    def project_in(t, carry):
-        tile = norm_columns(update(t, 0)).astype(BF)
-        mask = mask_at(mask_r, t)
-        for h in range(2):
-            put_arms(wall[h, n_first : 2 * n_first], h, tile, mask, t)
-        gate[:, span(t, width)] = jax.nn.sigmoid(dot(w_gate[1], tile, (1, 0)))
+
+    def lay_out(m, a):
+        tiles = [
+            recv_out[pl.ds((2 * m + k) * ncp, ncp), a].astype(F32).reshape(ncp * q_rows, lanes)
+            for k in range(2)
+        ]
+        low = jnp.where(left, tiles[0], pltpu.roll(tiles[1], block_i, 1))
+        high = jnp.where(left, pltpu.roll(tiles[0], block_i, 1), tiles[1])
+        both = [y.reshape(ncp, 1, q_rows, lanes) for y in (low, high)]
+        return jnp.concatenate(both, axis=1).reshape(n_tok, lanes).astype(BF)
+
+    for m in range(4):
+        arm_b[:, m * lanes : (m + 1) * lanes] = lay_out(m, 1)
+    mix_and_return(lambda m: lay_out(m, 0), back_out, home_out, 3, load_rows)
+
+    own_half = me // hdev
+
+    def in_half(h, first):
+        w = wall[pl.ds(h, 1), n_first : 2 * n_first, :].reshape(n_first, n_ch)
+
+        def body(t, carry):
+            if first:
+                tile = norm_columns(update(t, 0)).astype(BF)
+                normed[:, span(t, width)] = tile
+            else:
+                tile = normed[:, span(t, width)]
+            put_arms(w, h, tile, mask_at(mask_r, t), t)
+            return carry
+
+        lax.fori_loop(0, TILES, body, 0)
+        pack_arms(send_in, h * half, half)
+
+        def send(s, carry):
+            to = h * hdev + lax.rem(me + s * STEP, hdev)
+            copy(send_in.at[to], recv_in.at[me], 4, to).start()
+            return carry
+
+        lax.fori_loop(1 if first else 0, hdev, send, 0)
+
+    in_half(own_half, True)
+    in_half(1 - own_half, False)
+    recv_in[pl.ds(me, 1)] = send_in[pl.ds(me, 1)]
+
+    def gate_in(t, carry):
+        at = span(t, width)
+        gate[:, at] = jax.nn.sigmoid(dot(w_gate[1], normed[:, at], (1, 0)))
         return carry
 
-    lax.fori_loop(0, TILES, project_in, 0)
-    pack_arms(send_in, 0, n_dev)
-    all_to_all(send_in, recv_in, 4)
+    lax.fori_loop(0, TILES, gate_in, 0)
     arrived(recv_in, 4)
     unpack(lambda t, n: recv_in[pl.ds(t * n, n), 0], st_a)
     unpack(lambda t, n: recv_in[pl.ds(t * n, n), 1], st_b)
@@ -343,7 +383,7 @@
         rows = pl.ds(g, n_tok, stride=GROUPS)
         arm_a[:, g * lanes : (g + 1) * lanes] = st_a[rows, :].astype(BF)
         arm_b[:, g * lanes : (g + 1) * lanes] = st_b[rows, :].astype(BF)
-    mix_and_return(False, back_in, home_in, 5)
+    mix_and_return(lambda m: arm_a[:, span(m, lanes)], back_in, home_in, 5, lambda: None)
 
     def bias_step(t, carry):
         tile = norm_columns(update(t, 1)).astype(BF)
@@ -515,16 +555,17 @@
             vm(pair_t, F32),
             vm((ROWS, n_tok, n_ch), BF),
             vm(pair_input.shape, BF),
-            pltpu.SemaphoreType.DMA((18,)),
-            pltpu.SemaphoreType.DMA((18,)),
+            pltpu.SemaphoreType.DMA((20,)),
+            pltpu.SemaphoreType.DMA((20,)),
         ],
         compiler_params=pltpu.CompilerParams(
             collective_id=0, has_side_effects=True, vmem_limit_bytes=56 * 2**20
         ),
         name="pair_update",
     )(
-        pair_input, token_mask[None, :], out_stack, in_stack, att_stack,
-        out_final, in_final, att_out, att_bias, out_gate, in_gate,
+        pair_input, token_mask[None, :],
+        jnp.swapaxes(out_stack, 1, 2), jnp.swapaxes(in_stack, 1, 2), jnp.swapaxes(att_stack, 1, 2),
+        out_final, in_final, att_out, att_bias.T, out_gate, in_gate,
     )
     return pair_input + update.astype(F32)
 

time: 138 us -> 128 us (0.928)
  Pallas kernels: 131 us -> 125 us
  local copies, waits for them, and re-layouts: 4.61 us -> 0.01 us
    pallas_call x1, Pallas kernels: 131 us -> 125 us  [on_device(): pl.pallas_call(functools.partial(kernel, (nr, nc, np_, heads)), out_shape...]
    unnamed x12 -> x2, local copies, waits for them, and re-layouts: 4.61 us -> 0.01 us
where the time goes in v2:
time: 128 us
  Pallas kernels  125 us (98%)
  other arithmetic  2.17 us (2%)
    pallas_call x1, Pallas kernels, on_device(): pl.pallas_call(functools.partial(kernel, (nr, nc, np_, heads)), out_shape...  125 us

profile of v2, /device:TPU:1, one launch (start us, length us, event | category | flops | bytes accessed | tf_op | source)
XLA Modules:
  0.0 127.6 jit_solution(10717316474794907238)
XLA Ops:
  0.0 0.0 copy-start
  0.0 125.4 %pair_update.1 = bf16[64,32,128]{2,1,0:T(8,128)(2,1)} custom-call(f32[64,32,128]{2,1,0:T(8,128)} %x_ref.1, s32[1,512]{1,0:T(1,128)} %bitcast.8, bf16[4,64,128]{2,1,0:T(8,128)(2,1)} %bitcast.5, bf16[4,64,128]{2,1,0:T(8,128)(2,1)} %bitcast.6, bf16[4,64,128]{2,1,0:T(8,128)(2,1)} %bitcast.7, bf16[64,128]{1,0:T(8,128)(2,1)} %of_ref.1, bf16[64,128]{1,0:T(8,128)(2,1)} %if_ref.1, ...), custom_call_target="tpu_custom_call" | custom-call | tf_op jit(solution)/shard_map/pair_update/pallas_call | solution.py:522
  125.4 0.0 copy-done
  125.5 2.2 %convert_add_fusion = f32[64,32,128]{2,1,0:T(8,128)} fusion(f32[64,32,128]{2,1,0:T(8,128)S(1)} %copy-done, bf16[64,32,128]{2,1,0:T(8,128)(2,1)} %pair_update.1), kind=kLoop, calls=%fused_computation | loop fusion | flops 524288 | bytes 2621440 | tf_op jit(solution)/shard_map/add | solution.py:570
Async XLA Ops:
  0.0 125.4 %copy-start = (f32[64,32,128]{2,1,0:T(8,128)S(1)}, f32[64,32,128]{2,1,0:T(8,128)}, u32[]{:S(2)}) copy-start(f32[64,32,128]{2,1,0:T(8,128)} %x_ref.1) | copy-start | bytes 3145732

commit v3 on v2

--- a/solution.py
+++ b/solution.py
@@ -61,6 +61,7 @@
     cp = c * np_ + p
     me = r * ncp + cp
     core, unit = lax.rem(r, 2), (r // 2) * ncp + cp
+    slot = core * hdev + unit
 
     barrier = pltpu.get_barrier_semaphore()
 
@@ -182,15 +183,16 @@
         lax.fori_loop(0, TILES, body, 0)
         pack_arms(send_out, h * half, half)
 
-    def send_half(h):
+    def send_half(send, recv, sem, h):
         def body(s, carry):
-            to = h * hdev + lax.rem(me + s * STEP, hdev)
-            copy(send_out.at[to], recv_out.at[me], 2, to).start()
+            other = lax.rem(unit + s * STEP, hdev)
+            to = ((other // ncp) * 2 + h) * ncp + lax.rem(other, ncp)
+            copy(send.at[h * hdev + other], recv.at[me], sem, to).start()
             return carry
 
         lax.fori_loop(1, hdev, body, 0)
 
-        @pl.when(me // hdev != h)
+        @pl.when(core != h)
         def _():
             body(0, 0)
 
@@ -215,11 +217,11 @@
         return both
 
     early = give(0, n_first, 8)
-    send_half(p)
+    send_half(send_out, recv_out, 2, p)
     for w_copy in early:
         w_copy.wait()
     out_half(1 - p)
-    send_half(1 - p)
+    send_half(send_out, recv_out, 2, 1 - p)
     late = give(n_first, w_send.shape[0] - n_first, 18)
 
     def send_rows(s, carry):
@@ -232,7 +234,7 @@
 
     lax.fori_loop(1, ncp, send_rows, 0)
     xr[:, pl.ds(cp * block_j, block_j), :] = xs[pl.ds(cp * ROWS, ROWS)]
-    recv_out[pl.ds(me, 1)] = send_out[pl.ds(me, 1)]
+    recv_out[pl.ds(me, 1)] = send_out[pl.ds(slot, 1)]
 
     def load_rows():
         for w_copy in late:
@@ -286,8 +288,10 @@
     def mix_and_return(arm_chunk, back, home, sem, meanwhile):
         n = n_tok // 4
         n_to = n_dev // 4
+        y, x, z_of = r // 2, c // np_, lax.rem(c, 2) * np_ + p
         for k in range(4):
-            m = lax.rem(r // 2 + k, 4)
+            ahead = lax.rem(k + x + z_of, 4)
+            m = lax.rem(jnp.where(lax.rem(y, 2) == 0, y + ahead, y + 4 - ahead), 4)
             mixed = dot(arm_chunk(m), arm_b[...], (0, 0))
             for g in range(GROUPS):
                 rows = pl.ds(m * (n * GROUPS) + g, n, stride=GROUPS)
@@ -300,11 +304,16 @@
 
             def body(s, carry, m=m):
                 to = m * n_to + lax.rem(me + s * STEP, n_to)
-                copy(back.at[to], home.at[me], sem, to).start()
+                copy(back.at[to], home.at[slot], sem, to).start()
                 return carry
 
-            lax.fori_loop(0 if k else 1, n_to, body, 0)
-        home[pl.ds(me, 1)] = back[pl.ds(me, 1)]
+            lax.fori_loop(1, n_to, body, 0)
+
+            @pl.when(m != y)
+            def _(body=body):
+                body(0, 0)
+
+        home[pl.ds(slot, 1)] = back[pl.ds(me, 1)]
         meanwhile()
         arrived(home, sem)
         m = n_dev // 8
@@ -342,8 +351,6 @@
         arm_b[:, m * lanes : (m + 1) * lanes] = lay_out(m, 1)
     mix_and_return(lambda m: lay_out(m, 0), back_out, home_out, 3, load_rows)
 
-    own_half = me // hdev
-
     def in_half(h, first):
         w = wall[pl.ds(h, 1), n_first : 2 * n_first, :].reshape(n_first, n_ch)
 
@@ -358,17 +365,11 @@
 
         lax.fori_loop(0, TILES, body, 0)
         pack_arms(send_in, h * half, half)
-
-        def send(s, carry):
-            to = h * hdev + lax.rem(me + s * STEP, hdev)
-            copy(send_in.at[to], recv_in.at[me], 4, to).start()
-            return carry
-
-        lax.fori_loop(1 if first else 0, hdev, send, 0)
-
-    in_half(own_half, True)
-    in_half(1 - own_half, False)
-    recv_in[pl.ds(me, 1)] = send_in[pl.ds(me, 1)]
+        send_half(send_in, recv_in, 4, h)
+
+    in_half(0, True)
+    in_half(1, False)
+    recv_in[pl.ds(me, 1)] = send_in[pl.ds(slot, 1)]
 
     def gate_in(t, carry):
         at = span(t, width)
@@ -424,8 +425,6 @@
 
     lax.fori_loop(0, TILES, qkvg, 0)
     sibling = (r + 1 - 2 * core) * ncp + cp
-    wide = n_tok // 2
-
     def forward(h):
         drain(bias_recv.at[h, 0, pl.ds(0, hdev - 1)], recv_sem.at[10 + h])
         out = copy(bias_recv.at[h, core], bias_recv.at[h, core], 14 + h, sibling)
@@ -434,7 +433,7 @@
 
     def finish(i):
         for t in range(TILES // ROWS):
-            at = pl.ds(pl.multiple_of(i * n_tok + t * width, width), width)
+            at = slice(i * n_tok + t * width, i * n_tok + (t + 1) * width)
             gated = (gate[:, at] * att[:, at]).astype(BF)
             total = delta[:, at] + dot(w_fin[2], gated, (1, 0))
             fin_send[i, t * width : (t + 1) * width, :] = total.T.astype(BF)
@@ -460,24 +459,25 @@
             bias_t[g * lanes : (g + 1) * lanes, :] = jnp.where(seen, tile, -1e30).T
         mine = slice(h * h_dim, (h + 1) * h_dim)
 
-        def body(i, carry):
-            keys = k_n[i]
-            vals = jnp.concatenate([v_t[mine, span(i, n_tok)], jnp.ones((16, n_tok), BF)], axis=0)
-            channel = lax.broadcasted_iota(jnp.int32, (n_ch, wide), 0)
-            chosen = (channel >= h * h_dim) & (channel < (h + 1) * h_dim)
-            for k in range(2):
-                at = pl.ds(pl.multiple_of(i * n_tok + k * wide, wide), wide)
-                query = jnp.where(chosen, q_t[:, at].astype(F32), 0.0).astype(BF)
-                scores = dot(keys, query, (1, 0)) + bias_t[:, k * wide : (k + 1) * wide]
-                peak = jnp.max(scores, axis=0, keepdims=True)
-                weights = jnp.exp2(scores - peak).astype(BF)
-                got = dot(vals, weights, (1, 0))
-                att[mine, at] = got[:h_dim] / got[h_dim : h_dim + 1]
+        channel = lax.broadcasted_iota(jnp.int32, (n_ch, n_tok), 0)
+        chosen = (channel >= h * h_dim) & (channel < (h + 1) * h_dim)
+
+        def scores_of(i):
+            query = q_t[:, i * n_tok : (i + 1) * n_tok].astype(F32)
+            return dot(k_n[i], jnp.where(chosen, query, 0.0).astype(BF), (1, 0)) + bias_t[...]
+
+        following = scores_of(0)
+        for i in range(ROWS):
+            scores = following
+            if i + 1 < ROWS:
+                following = scores_of(i + 1)
+            at = slice(i * n_tok, (i + 1) * n_tok)
+            vals = jnp.concatenate([v_t[mine, at], jnp.ones((16, n_tok), BF)], axis=0)
+            peak = jnp.max(scores, axis=0, keepdims=True)
+            got = dot(vals, jnp.exp2(scores - peak).astype(BF), (1, 0))
+            att[mine, at] = got[:h_dim] / got[h_dim : h_dim + 1]
             if h == heads - 1:
                 finish(i)
-            return carry
-
-        lax.fori_loop(0, ROWS, body, 0)
 
     forwards = [forward(0)]
     for h in range(heads):

time: 128 us -> 106 us (0.83)
  Pallas kernels: 125 us -> 104 us
    pallas_call x1, Pallas kernels: 125 us -> 104 us  [on_device(): pl.pallas_call(functools.partial(kernel, (nr, nc, np_, heads)), out_shape...]
where the time goes in v3:
time: 106 us
  Pallas kernels  104 us (98%)
  other arithmetic  2.17 us (2%)
    pallas_call x1, Pallas kernels, on_device(): pl.pallas_call(functools.partial(kernel, (nr, nc, np_, heads)), out_shape...  104 us
    add x1, other arithmetic, on_device(): return pair_input + update.astype(F32)  2.17 us

profile of v3, /device:TPU:1, one launch (start us, length us, event | category | flops | bytes accessed | tf_op | source)
XLA Modules:
  0.0 106.2 jit_solution(9096131380524114469)
XLA Ops:
  0.0 0.0 copy-start
  0.0 104.0 %pair_update.1 = bf16[64,32,128]{2,1,0:T(8,128)(2,1)} custom-call(f32[64,32,128]{2,1,0:T(8,128)} %x_ref.1, s32[1,512]{1,0:T(1,128)} %bitcast.8, bf16[4,64,128]{2,1,0:T(8,128)(2,1)} %bitcast.5, bf16[4,64,128]{2,1,0:T(8,128)(2,1)} %bitcast.6, bf16[4,64,128]{2,1,0:T(8,128)(2,1)} %bitcast.7, bf16[64,128]{1,0:T(8,128)(2,1)} %of_ref.1, bf16[64,128]{1,0:T(8,128)(2,1)} %if_ref.1, ...), custom_call_target="tpu_custom_call" | custom-call | tf_op jit(solution)/shard_map/pair_update/pallas_call | solution.py:522
  104.0 0.0 copy-done
  104.1 2.2 %convert_add_fusion = f32[64,32,128]{2,1,0:T(8,128)} fusion(f32[64,32,128]{2,1,0:T(8,128)S(1)} %copy-done, bf16[64,32,128]{2,1,0:T(8,128)(2,1)} %pair_update.1), kind=kLoop, calls=%fused_computation | loop fusion | flops 524288 | bytes 2621440 | tf_op jit(solution)/shard_map/add | solution.py:570
Async XLA Ops:
  0.0 104.0 %copy-start = (f32[64,32,128]{2,1,0:T(8,128)S(1)}, f32[64,32,128]{2,1,0:T(8,128)}, u32[]{:S(2)}) copy-start(f32[64,32,128]{2,1,0:T(8,128)} %x_ref.1) | copy-start | bytes 3145732

commit v4 on v3

--- a/solution.py
+++ b/solution.py
@@ -21,6 +21,11 @@
 
 def dot(a, b, contract):
     return lax.dot_general(a, b, ((contract[:1], contract[1:]), ((), ())), preferred_element_type=F32)
+
+
+def steps(count, body):
+    for t in range(count):
+        body(t)
 
 
 def norm_columns(x):
@@ -84,7 +89,8 @@
         pltpu.make_async_copy(ref, ref, sem).wait()
 
     def span(t, size):
-        return pl.ds(pl.multiple_of(t * size, size), size)
+        at = t * size
+        return pl.ds(at if isinstance(at, int) else pl.multiple_of(at, size), size)
 
     n_first = 4 * half
     base = 3 * n_first
@@ -125,7 +131,7 @@
     xs[...] = x_ref[...].astype(BF)
     st_a[...] = x_ref[...].reshape(block_i * block_j, n_ch)
 
-    def norm_input(t, carry):
+    def norm_input(t):
         tile = jnp.concatenate(
             [
                 st_a[pl.ds(e * q_rows + t * per + k, block_i, stride=block_j), :]
@@ -135,9 +141,8 @@
             axis=0,
         )
         normed[:, span(t, width)] = norm_columns(tile.T).astype(BF)
-        return carry
-
-    lax.fori_loop(0, TILES, norm_input, 0)
+
+    steps(TILES, norm_input)
 
     def put_arms(w, h, tile, mask, t):
         proj = dot(w, tile, (1, 0))
@@ -155,13 +160,15 @@
     def pack(src, first, count, store):
         n = max(count // 8, 1)
 
-        def body(t, carry):
+        def body(t):
             at = first + t * n
-            rows = pl.ds(pl.multiple_of(at * q_rows, n * q_rows), n * q_rows)
+            start = at * q_rows
+            if not isinstance(at, int):
+                start = pl.multiple_of(start, n * q_rows)
+            rows = pl.ds(start, n * q_rows)
             store(pl.ds(at, n), src[rows, :].reshape(n, q_rows, lanes).astype(BF))
-            return carry
-
-        lax.fori_loop(0, count // n, body, 0)
+
+        steps(count // n, body)
 
     def pack_arms(send, first, count):
         def store_first(at, tile):
@@ -176,11 +183,10 @@
     def out_half(h):
         w = wall[pl.ds(h, 1), :n_first, :].reshape(n_first, n_ch)
 
-        def body(t, carry):
+        def body(t):
             put_arms(w, h, normed[:, span(t, width)], mask_at(mask_o, t), t)
-            return carry
-
-        lax.fori_loop(0, TILES, body, 0)
+
+        steps(TILES, body)
         pack_arms(send_out, h * half, half)
 
     def send_half(send, recv, sem, h):
@@ -251,25 +257,23 @@
         ).astype(BF)
         drain(xs.at[pl.ds(0, (ncp - 1) * ROWS)], recv_sem.at[1])
 
-        def load_state(t, carry):
+        def load_state(t):
             at = span(t, width)
-            row, off = t // (TILES // ROWS), lax.rem(t, TILES // ROWS)
+            row, off = t // (TILES // ROWS), t % (TILES // ROWS)
             tile = xr[row, span(off, width), :].astype(F32).T
             state[:, at] = tile
             gate[:, at] = jax.nn.sigmoid(dot(w_gate[0], norm_columns(tile).astype(BF), (1, 0)))
-            return carry
-
-        lax.fori_loop(0, TILES, load_state, 0)
+
+        steps(TILES, load_state)
 
     def unpack(load, dst):
         n = n_dev // 8
 
-        def body(t, carry):
+        def body(t):
             tile = load(t, n).astype(F32).reshape(n * q_rows, lanes)
             dst[span(t, n * q_rows), :] = tile
-            return carry
-
-        lax.fori_loop(0, 8, body, 0)
+
+        steps(8, body)
 
     def arrived(dst, sem):
         drain(dst.at[pl.ds(0, n_dev - 1)], recv_sem.at[sem])
@@ -323,16 +327,17 @@
             return carry[0] + jnp.sum(tile, axis=0), carry[1] + jnp.sum(tile * tile, axis=0)
 
         zero = jnp.zeros((q_rows, lanes), F32)
-        total, squares = lax.fori_loop(0, 8, sums, (zero, zero))
+        total, squares = zero, zero
+        for t in range(8):
+            total, squares = sums(t, (total, squares))
         mean = total / n_ch
         scale = lax.rsqrt(squares / n_ch - mean * mean + EPS)
 
-        def normalize(t, carry):
+        def normalize(t):
             tile = (home[pl.ds(t * m, m)].astype(F32) - mean[None]) * scale[None]
             st_a[span(t, m * q_rows), :] = tile.reshape(m * q_rows, lanes)
-            return carry
-
-        lax.fori_loop(0, 8, normalize, 0)
+
+        steps(8, normalize)
 
     arrived(recv_out, 2)
     left = lax.broadcasted_iota(jnp.int32, (ncp * q_rows, lanes), 1) < block_i
@@ -354,16 +359,15 @@
     def in_half(h, first):
         w = wall[pl.ds(h, 1), n_first : 2 * n_first, :].reshape(n_first, n_ch)
 
-        def body(t, carry):
+        def body(t):
             if first:
                 tile = norm_columns(update(t, 0)).astype(BF)
                 normed[:, span(t, width)] = tile
             else:
                 tile = normed[:, span(t, width)]
             put_arms(w, h, tile, mask_at(mask_r, t), t)
-            return carry
-
-        lax.fori_loop(0, TILES, body, 0)
+
+        steps(TILES, body)
         pack_arms(send_in, h * half, half)
         send_half(send_in, recv_in, 4, h)
 
@@ -371,12 +375,11 @@
     in_half(1, False)
     recv_in[pl.ds(me, 1)] = send_in[pl.ds(slot, 1)]
 
-    def gate_in(t, carry):
+    def gate_in(t):
         at = span(t, width)
         gate[:, at] = jax.nn.sigmoid(dot(w_gate[1], normed[:, at], (1, 0)))
-        return carry
-
-    lax.fori_loop(0, TILES, gate_in, 0)
+
+    steps(TILES, gate_in)
     arrived(recv_in, 4)
     unpack(lambda t, n: recv_in[pl.ds(t * n, n), 0], st_a)
     unpack(lambda t, n: recv_in[pl.ds(t * n, n), 1], st_b)
@@ -386,15 +389,14 @@
         arm_b[:, g * lanes : (g + 1) * lanes] = st_b[rows, :].astype(BF)
     mix_and_return(lambda m: arm_a[:, span(m, lanes)], back_in, home_in, 5, lambda: None)
 
-    def bias_step(t, carry):
+    def bias_step(t):
         tile = norm_columns(update(t, 1)).astype(BF)
         normed[:, span(t, width)] = tile
         proj = dot(w_bias[...], tile, (1, 0)) * LOG2E
         for k in range(per):
             bias_st[pl.ds(t * per + k, 8, stride=q_rows), :] = proj[:, k * lanes : (k + 1) * lanes]
-        return carry
-
-    lax.fori_loop(0, TILES, bias_step, 0)
+
+    steps(TILES, bias_step)
     bias_send[...] = bias_st[: heads * q_rows].astype(BF).reshape(heads, q_rows, lanes)
     for h in range(heads):
 
@@ -407,10 +409,10 @@
         lax.fori_loop(1, hdev, send_bias, 0)
         bias_recv[h, pl.ds(core, 1), pl.ds(unit, 1)] = bias_send[h][None, None]
 
-    def qkvg(t, carry):
+    def qkvg(t):
         at = span(t, width)
         tile = normed[:, at]
-        row, off = t // (TILES // ROWS), lax.rem(t, TILES // ROWS)
+        row, off = t // (TILES // ROWS), t % (TILES // ROWS)
         keys = []
         m = half
         for h in range(2):
@@ -421,9 +423,8 @@
             v_t[mine, at] = proj[2 * m : 3 * m].astype(BF)
             gate[mine, at] = jax.nn.sigmoid(proj[3 * m :])
         k_n[row, span(off, width), :] = jnp.concatenate(keys, axis=0).T.astype(BF)
-        return carry
-
-    lax.fori_loop(0, TILES, qkvg, 0)
+
+    steps(TILES, qkvg)
     sibling = (r + 1 - 2 * core) * ncp + cp
     def forward(h):
         drain(bias_recv.at[h, 0, pl.ds(0, hdev - 1)], recv_sem.at[10 + h])
@@ -450,7 +451,7 @@
 
     def attend(h):
         def load(t, n):
-            return bias_recv[h, pl.ds(lax.rem(t, 2), 1), pl.ds(t // 2 * n, n)].reshape(n, q_rows, lanes)
+            return bias_recv[h, pl.ds(t % 2, 1), pl.ds(t // 2 * n, n)].reshape(n, q_rows, lanes)
 
         unpack(load, st_a)
         for g in range(GROUPS):

time: 106 us -> 102 us (0.962)
  Pallas kernels: 104 us -> 99.9 us
    pallas_call x1, Pallas kernels: 104 us -> 99.9 us  [on_device(): pl.pallas_call(functools.partial(kernel, (nr, nc, np_, heads)), out_shape...]
where the time goes in v4:
time: 102 us
  Pallas kernels  99.9 us (98%)
  other arithmetic  2.17 us (2%)
    pallas_call x1, Pallas kernels, on_device(): pl.pallas_call(functools.partial(kernel, (nr, nc, np_, heads)), out_shape...  99.9 us
    add x1, other arithmetic, on_device(): return pair_input + update.astype(F32)  2.17 us

profile of v4, /device:TPU:1, one launch (start us, length us, event | category | flops | bytes accessed | tf_op | source)
XLA Modules:
  0.0 102.1 jit_solution(9867454551629435004)
XLA Ops:
  0.0 0.0 copy-start
  0.0 99.9 %pair_update.1 = bf16[64,32,128]{2,1,0:T(8,128)(2,1)} custom-call(f32[64,32,128]{2,1,0:T(8,128)} %x_ref.1, s32[1,512]{1,0:T(1,128)} %bitcast.8, bf16[4,64,128]{2,1,0:T(8,128)(2,1)} %bitcast.5, bf16[4,64,128]{2,1,0:T(8,128)(2,1)} %bitcast.6, bf16[4,64,128]{2,1,0:T(8,128)(2,1)} %bitcast.7, bf16[64,128]{1,0:T(8,128)(2,1)} %of_ref.1, bf16[64,128]{1,0:T(8,128)(2,1)} %if_ref.1, ...), custom_call_target="tpu_custom_call" | custom-call | tf_op jit(solution)/shard_map/pair_update/pallas_call | solution.py:523
  99.9 0.0 copy-done
  99.9 2.2 %convert_add_fusion = f32[64,32,128]{2,1,0:T(8,128)} fusion(f32[64,32,128]{2,1,0:T(8,128)S(1)} %copy-done, bf16[64,32,128]{2,1,0:T(8,128)(2,1)} %pair_update.1), kind=kLoop, calls=%fused_computation | loop fusion | flops 524288 | bytes 2621440 | tf_op jit(solution)/shard_map/add | solution.py:571
Async XLA Ops:
  0.0 99.9 %copy-start = (f32[64,32,128]{2,1,0:T(8,128)S(1)}, f32[64,32,128]{2,1,0:T(8,128)}, u32[]{:S(2)}) copy-start(f32[64,32,128]{2,1,0:T(8,128)} %x_ref.1) | copy-start | bytes 3145732

commit v5 on v4

--- a/solution.py
+++ b/solution.py
@@ -16,7 +16,7 @@
 ROWS = 4
 GROUPS = 4
 TILES = 8
-STEP = 45
+STEP = 21
 
 
 def dot(a, b, contract):
@@ -71,7 +71,11 @@
     barrier = pltpu.get_barrier_semaphore()
 
     def place(to):
-        return to // ncp, lax.rem(to, ncp) // np_, lax.rem(to, np_)
+        return lax.div(to, ncp), lax.div(lax.rem(to, ncp), np_), lax.rem(to, np_)
+
+    def at_unit(other, k):
+        col = lax.div(lax.rem(other, ncp), np_)
+        return lax.div(other, ncp) * 2 + k, col, lax.rem(other, np_)
 
     for s in range(1, n_dev):
         s = s * STEP % n_dev
@@ -82,7 +86,7 @@
     def copy(src, dst, sem, to):
         return pltpu.make_async_remote_copy(
             src_ref=src, dst_ref=dst, send_sem=send_sem.at[sem], recv_sem=recv_sem.at[sem],
-            device_id=place(to), device_id_type=MESH,
+            device_id=to if isinstance(to, tuple) else place(to), device_id_type=MESH,
         )
 
     def drain(ref, sem):
@@ -192,8 +196,7 @@
     def send_half(send, recv, sem, h):
         def body(s, carry):
             other = lax.rem(unit + s * STEP, hdev)
-            to = ((other // ncp) * 2 + h) * ncp + lax.rem(other, ncp)
-            copy(send.at[h * hdev + other], recv.at[me], sem, to).start()
+            copy(send.at[h * hdev + other], recv.at[me], sem, at_unit(other, h)).start()
             return carry
 
         lax.fori_loop(1, hdev, body, 0)
@@ -402,8 +405,7 @@
 
         def send_bias(s, carry, h=h):
             other = lax.rem(unit + s * STEP, hdev)
-            to = ((other // ncp) * 2 + core) * ncp + lax.rem(other, ncp)
-            copy(bias_send.at[h], bias_recv.at[h, core, unit], 10 + h, to).start()
+            copy(bias_send.at[h], bias_recv.at[h, core, unit], 10 + h, at_unit(other, core)).start()
             return carry
 
         lax.fori_loop(1, hdev, send_bias, 0)

time: 102 us -> 101 us (level)
  no operation moved by 1% of the time
where the time goes in v5:
time: 101 us
  Pallas kernels  98.9 us (98%)
  other arithmetic  2.17 us (2%)
    pallas_call x1, Pallas kernels, on_device(): pl.pallas_call(functools.partial(kernel, (nr, nc, np_, heads)), out_shape...  98.9 us
    add x1, other arithmetic, on_device(): return pair_input + update.astype(F32)  2.17 us

profile of v5, /device:TPU:1, one launch (start us, length us, event | category | flops | bytes accessed | tf_op | source)
XLA Modules:
  0.0 101.1 jit_solution(15309660542879448063)
XLA Ops:
  0.0 0.0 copy-start
  0.0 98.9 %pair_update.1 = bf16[64,32,128]{2,1,0:T(8,128)(2,1)} custom-call(f32[64,32,128]{2,1,0:T(8,128)} %x_ref.1, s32[1,512]{1,0:T(1,128)} %bitcast.8, bf16[4,64,128]{2,1,0:T(8,128)(2,1)} %bitcast.5, bf16[4,64,128]{2,1,0:T(8,128)(2,1)} %bitcast.6, bf16[4,64,128]{2,1,0:T(8,128)(2,1)} %bitcast.7, bf16[64,128]{1,0:T(8,128)(2,1)} %of_ref.1, bf16[64,128]{1,0:T(8,128)(2,1)} %if_ref.1, ...), custom_call_target="tpu_custom_call" | custom-call | tf_op jit(solution)/shard_map/pair_update/pallas_call | solution.py:525
  98.9 0.0 copy-done
  98.9 2.2 %convert_add_fusion = f32[64,32,128]{2,1,0:T(8,128)} fusion(f32[64,32,128]{2,1,0:T(8,128)S(1)} %copy-done, bf16[64,32,128]{2,1,0:T(8,128)(2,1)} %pair_update.1), kind=kLoop, calls=%fused_computation | loop fusion | flops 524288 | bytes 2621440 | tf_op jit(solution)/shard_map/add | solution.py:573
Async XLA Ops:
  0.0 98.9 %copy-start = (f32[64,32,128]{2,1,0:T(8,128)S(1)}, f32[64,32,128]{2,1,0:T(8,128)}, u32[]{:S(2)}) copy-start(f32[64,32,128]{2,1,0:T(8,128)} %x_ref.1) | copy-start | bytes 3145732

commit v6 on v5

--- a/solution.py
+++ b/solution.py
@@ -401,7 +401,7 @@
 
     steps(TILES, bias_step)
     bias_send[...] = bias_st[: heads * q_rows].astype(BF).reshape(heads, q_rows, lanes)
-    for h in range(heads):
+    def send_head(h):
 
         def send_bias(s, carry, h=h):
             other = lax.rem(unit + s * STEP, hdev)
@@ -426,7 +426,11 @@
             gate[mine, at] = jax.nn.sigmoid(proj[3 * m :])
         k_n[row, span(off, width), :] = jnp.concatenate(keys, axis=0).T.astype(BF)
 
+    send_head(0)
+    send_head(1)
     steps(TILES, qkvg)
+    send_head(2)
+    send_head(3)
     sibling = (r + 1 - 2 * core) * ncp + cp
     def forward(h):
         drain(bias_recv.at[h, 0, pl.ds(0, hdev - 1)], recv_sem.at[10 + h])

time: 101 us -> 101 us (level)
  no operation moved by 1% of the time
where the time goes in v6:
time: 101 us
  Pallas kernels  98.9 us (98%)
  other arithmetic  2.17 us (2%)
    pallas_call x1, Pallas kernels, on_device(): pl.pallas_call(functools.partial(kernel, (nr, nc, np_, heads)), out_shape...  98.9 us
    add x1, other arithmetic, on_device(): return pair_input + update.astype(F32)  2.17 us

profile of v6, /device:TPU:1, one launch (start us, length us, event | category | flops | bytes accessed | tf_op | source)
XLA Modules:
  0.0 101.1 jit_solution(3460160360515112974)
XLA Ops:
  0.0 0.0 copy-start
  0.0 98.9 %pair_update.1 = bf16[64,32,128]{2,1,0:T(8,128)(2,1)} custom-call(f32[64,32,128]{2,1,0:T(8,128)} %x_ref.1, s32[1,512]{1,0:T(1,128)} %bitcast.8, bf16[4,64,128]{2,1,0:T(8,128)(2,1)} %bitcast.5, bf16[4,64,128]{2,1,0:T(8,128)(2,1)} %bitcast.6, bf16[4,64,128]{2,1,0:T(8,128)(2,1)} %bitcast.7, bf16[64,128]{1,0:T(8,128)(2,1)} %of_ref.1, bf16[64,128]{1,0:T(8,128)(2,1)} %if_ref.1, ...), custom_call_target="tpu_custom_call" | custom-call | tf_op jit(solution)/shard_map/pair_update/pallas_call | solution.py:529
  98.9 0.0 copy-done
  98.9 2.2 %convert_add_fusion = f32[64,32,128]{2,1,0:T(8,128)} fusion(f32[64,32,128]{2,1,0:T(8,128)S(1)} %copy-done, bf16[64,32,128]{2,1,0:T(8,128)(2,1)} %pair_update.1), kind=kLoop, calls=%fused_computation | loop fusion | flops 524288 | bytes 2621440 | tf_op jit(solution)/shard_map/add | solution.py:577
Async XLA Ops:
  0.0 98.9 %copy-start = (f32[64,32,128]{2,1,0:T(8,128)S(1)}, f32[64,32,128]{2,1,0:T(8,128)}, u32[]{:S(2)}) copy-start(f32[64,32,128]{2,1,0:T(8,128)} %x_ref.1) | copy-start | bytes 3145732
